TPU v7x, 256 devices: a whole 4x4x8 slice. The times are simulated.
256 devices in a mesh: group: 16 (over y_hi, x, core), tp: 16 (over y_lo, z).
Axes of the slice: x: 4, y: 4 (y_hi: 2, y_lo: 2; y = y_hi * 2 + y_lo), z: 8, core: 2. Of those that a mesh axis runs over, the one named last changes fastest.
Arguments:
- layer_inputs: bfloat16 [128, 4, 5120], P('group'), may hold values from -6 to 6
- input_norm_gain: bfloat16 [5120], replicated, may hold values from 0.099609375 to 1.8984375
- query_norm_gain: bfloat16 [128], replicated, may hold values from 1 to 2
- key_norm_gain: bfloat16 [128], replicated, may hold values from 1 to 2
- query_matrix: bfloat16 [5120, 4096], P(None, 'tp'), may hold values from -0.078125 to 0.078125
- key_matrix: bfloat16 [5120, 512], P(None, 'tp'), may hold values from -0.078125 to 0.078125
- value_matrix: bfloat16 [5120, 512], P(None, 'tp'), may hold values from -0.078125 to 0.078125
- output_matrix: bfloat16 [4096, 5120], P('tp'), may hold values from -0.09375 to 0.09375
- adapter_down: bfloat16 [5120, 192], P('group', 'tp'), may hold values from -0.078125 to 0.078125
- query_up_factor: bfloat16 [64, 4096], P('group', 'tp'), may hold values from -0.119628906 to 0.119628906
- key_up_factor: bfloat16 [64, 512], P('group', 'tp'), may hold values from -0.119628906 to 0.119628906
- value_up_factor: bfloat16 [64, 512], P('group', 'tp'), may hold values from -0.119628906 to 0.119628906
- output_down_factor: bfloat16 [4096, 64], P('tp', 'group'), may hold values from -0.09375 to 0.09375
- output_up_factor: bfloat16 [64, 5120], P('group', 'tp'), may hold values from -0.119628906 to 0.119628906
- stored_keys: bfloat16 [128, 2048, 512], P('group', 'tp'), may hold values from -120 to 120
- stored_values: bfloat16 [128, 2048, 512], P('group', 'tp'), may hold values from -12 to 12
- filled_lengths: int32 [128], P('group'), may hold values from 1 to 2048, as said below
Outputs:
- attn_output: bfloat16 [128, 4, 5120], P('group', None, 'tp')
Inputs may be any that keep to these rules, and one draw needn't show every extreme that they name: `filled_lengths`: some row's cache is full.
All inputs are finite; a program needn't handle non-finite values.
Results may differ from a plain program's by a relative error of at most 0.025.
Values may be sent and summed in bfloat16 or wider, within the bound.
No kernel may reach another device: no remote copies, remote signals or barrier semaphores. Data moves between devices by JAX's collectives and lax.ppermute only.
A program may use at most 128 MiB of HBM per device.

v0:
```python
import math

import jax
import jax.numpy as jnp
from jax import lax
from jax.sharding import PartitionSpec as P

EPS = 1e-06
ADAPTER_SCALE = 2.0
THETA = 1000000.0


def merged(value, axis, join):
    pieces = jax.tree.map(lambda part: lax.all_gather(part, axis), value)
    head = jax.tree.map(lambda part: part[0], pieces)
    tail = jax.tree.map(lambda part: part[1:], pieces)
    running, _ = lax.scan(lambda running, piece: (join(running, piece), None), head, tail)
    return running


def rms_scale(values):
    return values * lax.rsqrt(jnp.mean(values * values, axis=-1, keepdims=True) + EPS)


def rotate(heads, positions):
    half_dim = heads.shape[-1] // 2
    inverse = THETA ** (-(jnp.arange(half_dim, dtype=jnp.float32) * 2.0 / heads.shape[-1]))
    angles = positions[..., None, None] * inverse
    cosines = jnp.cos(angles)
    sines = jnp.sin(angles)
    leading = heads[..., :half_dim]
    trailing = heads[..., half_dim:]
    return jnp.concatenate(
        [leading * cosines - trailing * sines, trailing * cosines + leading * sines], axis=-1
    )


def merge_adapter(base_weight, lower, upper):
    weight_update = jnp.dot(lower, upper, preferred_element_type=jnp.float32)
    return (base_weight.astype(jnp.float32) + ADAPTER_SCALE * weight_update).astype(jnp.bfloat16)


def project(
    layer_inputs,
    input_norm_gain,
    query_norm_gain,
    query_merged_weight,
    key_merged_weight,
    value_merged_weight,
    lengths,
):
    rows_here, step_count, width = layer_inputs.shape
    head_dim = query_norm_gain.shape[0]
    flat = layer_inputs.astype(jnp.float32).reshape(rows_here * step_count, width)
    normed = (rms_scale(flat) * input_norm_gain.astype(jnp.float32)).astype(jnp.bfloat16)
    positions = (lengths[:, None] + jnp.arange(step_count, dtype=jnp.int32)[None, :]).astype(
        jnp.float32
    )
    raw_queries = jnp.dot(normed, query_merged_weight, preferred_element_type=jnp.float32).reshape(
        rows_here, step_count, -1, head_dim
    )
    queries = rotate(rms_scale(raw_queries) * query_norm_gain.astype(jnp.float32), positions)
    queries = queries.astype(jnp.bfloat16).reshape(rows_here, step_count, -1)
    raw_keys = (
        jnp.dot(normed, key_merged_weight, preferred_element_type=jnp.float32)
        .astype(jnp.bfloat16)
        .reshape(rows_here, step_count, -1)
    )
    new_values = (
        jnp.dot(normed, value_merged_weight, preferred_element_type=jnp.float32)
        .astype(jnp.bfloat16)
        .reshape(rows_here, step_count, -1)
    )
    return (queries, raw_keys, new_values, positions)


def finish_keys(raw_keys, positions, head_dim, key_norm_gain):
    rows_here, step_count, _ = raw_keys.shape
    heads = raw_keys.astype(jnp.float32).reshape(rows_here, step_count, -1, head_dim)
    return (
        rotate(rms_scale(heads) * key_norm_gain.astype(jnp.float32), positions)
        .astype(jnp.bfloat16)
        .reshape(rows_here, step_count, -1)
    )


def partial_softmax(
    all_queries, new_keys, all_values, stored_keys, stored_values, lengths, offset, leader, head_dim
):
    rows_here, step_count, _ = all_queries.shape
    kv_heads = new_keys.shape[-1] // head_dim
    span_local = stored_keys.shape[1]
    joined_keys = jnp.concatenate([stored_keys, new_keys], axis=1).reshape(
        rows_here, -1, kv_heads, head_dim
    )
    joined_values = jnp.concatenate([stored_values, all_values], axis=1).reshape(
        rows_here, -1, kv_heads, head_dim
    )
    query_groups = all_queries.reshape(rows_here, step_count, kv_heads, -1, head_dim)
    scores = jnp.einsum(
        "bsngd,bknd->bngsk", query_groups, joined_keys, preferred_element_type=jnp.float32
    ) / math.sqrt(head_dim)
    position = jnp.arange(span_local + step_count, dtype=jnp.int32)
    in_cache = position[None, :] + offset < lengths[:, None]
    causal = position[None, :] - span_local <= jnp.arange(step_count, dtype=jnp.int32)[:, None]
    usable = jnp.where(
        position[None, None, :] < span_local,
        in_cache[:, None, :],
        jnp.logical_and(causal[None], leader),
    )
    usable = usable[:, None, None]
    masked = jnp.where(usable, scores, -1e30)
    maxima = jnp.max(masked, axis=-1)
    weights = jnp.where(usable, jnp.exp(masked - maxima[..., None]), 0.0).astype(jnp.bfloat16)
    totals = jnp.sum(weights.astype(jnp.float32), axis=-1)
    weighted = jnp.einsum(
        "bngsk,bknd->bngsd", weights, joined_values, preferred_element_type=jnp.float32
    )
    maxima = maxima.transpose(0, 3, 1, 2).reshape(rows_here, step_count, -1)
    totals = totals.transpose(0, 3, 1, 2).reshape(rows_here, step_count, -1)
    weighted = weighted.transpose(0, 3, 1, 2, 4).reshape(rows_here, step_count, -1, head_dim)
    return (maxima, totals, weighted)


def blend(earlier, later):
    maxima_a, totals_a, weighted_a = earlier
    maxima_b, totals_b, weighted_b = later
    highest = jnp.maximum(maxima_a, maxima_b)
    factor_a = jnp.exp(maxima_a - highest)
    factor_b = jnp.exp(maxima_b - highest)
    return (
        highest,
        totals_a * factor_a + totals_b * factor_b,
        weighted_a * factor_a[..., None] + weighted_b * factor_b[..., None],
    )


def local(
    layer_inputs,
    input_norm_gain,
    query_norm_gain,
    key_norm_gain,
    query_matrix,
    key_matrix,
    value_matrix,
    output_matrix,
    adapter_down,
    query_up_factor,
    key_up_factor,
    value_up_factor,
    output_down_factor,
    output_up_factor,
    stored_keys,
    stored_values,
    filled_lengths,
):
    down_rows, query_lift, key_lift, value_lift, out_lower, lift_rows = (
        lax.all_gather(adapter_down, "group", axis=0, tiled=True),
        lax.all_gather(query_up_factor, "group", axis=0, tiled=True),
        lax.all_gather(key_up_factor, "group", axis=0, tiled=True),
        lax.all_gather(value_up_factor, "group", axis=0, tiled=True),
        lax.all_gather(output_down_factor, "group", axis=1, tiled=True),
        lax.all_gather(output_up_factor, "group", axis=0, tiled=True),
    )
    down_full, out_lift = (
        lax.all_gather(down_rows, "tp", axis=1, tiled=True),
        lax.all_gather(lift_rows, "tp", axis=1, tiled=True),
    )
    factor_rank = query_lift.shape[0]
    query_merged_weight = merge_adapter(query_matrix, down_full[:, :factor_rank], query_lift)
    key_merged_weight = merge_adapter(
        key_matrix, down_full[:, factor_rank : 2 * factor_rank], key_lift
    )
    value_merged_weight = merge_adapter(value_matrix, down_full[:, 2 * factor_rank :], value_lift)
    merged_output = merge_adapter(output_matrix, out_lower, out_lift)
    head_dim = query_norm_gain.shape[0]
    queries, raw_keys, new_values, positions = project(
        layer_inputs,
        input_norm_gain,
        query_norm_gain,
        query_merged_weight,
        key_merged_weight,
        value_merged_weight,
        filled_lengths,
    )
    all_queries, all_raw_keys, all_values = (
        lax.all_gather(queries, "tp", axis=2, tiled=True),
        lax.all_gather(raw_keys, "tp", axis=2, tiled=True),
        lax.all_gather(new_values, "tp", axis=2, tiled=True),
    )
    new_keys = finish_keys(all_raw_keys, positions, head_dim, key_norm_gain)
    leader = lax.axis_index("tp") == 0
    offset = lax.axis_index("tp") * stored_keys.shape[1]
    maxima, totals, weighted = partial_softmax(
        all_queries,
        new_keys,
        all_values,
        stored_keys,
        stored_values,
        filled_lengths,
        offset,
        leader,
        head_dim,
    )
    own_heads = queries.shape[2] // head_dim
    head_start = lax.axis_index("tp") * own_heads
    rows_here, step_count, _ = layer_inputs.shape
    maxima, totals, weighted = merged((maxima, totals, weighted), "tp", blend)
    every_head = (weighted / totals[..., None]).astype(jnp.bfloat16)
    heads_out = lax.dynamic_slice_in_dim(every_head, head_start, own_heads, 2).reshape(
        rows_here * step_count, -1
    )
    every_head = every_head.reshape(rows_here * step_count, -1)
    partial_value = jnp.dot(heads_out, merged_output, preferred_element_type=jnp.float32).reshape(
        rows_here, step_count, -1
    )
    return lax.psum_scatter(
        partial_value.astype(jnp.bfloat16), "tp", scatter_dimension=2, tiled=True
    )


def solution(mesh):
    in_specs = (
        P("group", None, None),
        P(),
        P(),
        P(),
        P(None, "tp"),
        P(None, "tp"),
        P(None, "tp"),
        P("tp", None),
        P("group", "tp"),
        P("group", "tp"),
        P("group", "tp"),
        P("group", "tp"),
        P("tp", "group"),
        P("group", "tp"),
        P("group", "tp", None),
        P("group", "tp", None),
        P("group"),
    )
    out_specs = P("group", None, "tp")
    return jax.shard_map(local, mesh=mesh, in_specs=in_specs, out_specs=out_specs, check_vma=False)
```

profile of v0, /device:TPU:2, one launch (start us, length us, event | category | flops | bytes accessed | tf_op | source)
XLA Modules:
  0.0 506.0 jit_solution(9363379088023262037)
XLA Ops:
  6.5 21.9 %all-gather = bf16[16,320,12]{1,2,0:T(8,128)(2,1)S(1)} all-gather(bf16[1,320,12]{1,2,0:T(8,128)(2,1)} %bitcast.134), channel_id=1, replica_groups=mesh['group'=16,'tp'=16] {'group'}, dimensions={0}, use_global_device_ids=true | all-gather | bytes 130560 | tf_op jit(solution)/shard_map/all_gather | solution.py:158
  29.5 3.0 copy.128
  32.5 22.7 %all-gather.3 = bf16[16,4,256]{2,1,0:T(4,128)(2,1)S(1)} all-gather(bf16[1,4,256]{2,1,0:T(4,128)(2,1)S(1)} %bitcast.138), channel_id=1, replica_groups=mesh['group'=16,'tp'=16] {'group'}, dimensions={0}, use_global_device_ids=true | all-gather | bytes 34816 | tf_op jit(solution)/shard_map/all_gather | solution.py:159
  57.1 2.3 copy.121
  59.4 2.3 copy.127
  61.8 2.8 copy.134
  64.6 19.3 %all-gather.2 = bf16[16,4,32]{2,1,0:T(4,128)(2,1)S(1)} all-gather(bf16[1,4,32]{2,1,0:T(4,128)(2,1)S(1)} %bitcast.140), channel_id=1, replica_groups=mesh['group'=16,'tp'=16] {'group'}, dimensions={0}, use_global_device_ids=true | all-gather | bytes 4352 | tf_op jit(solution)/shard_map/all_gather | solution.py:160
  83.8 22.0 %all-gather.4 = bf16[16,4,32]{2,1,0:T(4,128)(2,1)} all-gather(bf16[1,4,32]{2,1,0:T(4,128)(2,1)S(1)} %bitcast.141), channel_id=1, replica_groups=mesh['group'=16,'tp'=16] {'group'}, dimensions={0}, use_global_device_ids=true | all-gather | bytes 4352 | tf_op jit(solution)/shard_map/all_gather | solution.py:161
  106.9 4.0 reshape.194
  110.9 2.0 fusion.6
  114.4 39.2 %all_gather.47 = bf16[8,4,4096]{2,0,1:T(8,128)(2,1)} all-gather(bf16[8,4,256]{2,0,1:T(8,128)(2,1)S(1)} %convert_element_type.88), channel_id=1, replica_groups=mesh['group'=16,'tp'=16] {'tp'}, dimensions={2}, use_global_device_ids=true | all-gather | bytes 278528 | tf_op jit(solution)/shard_map/all_gather | solution.py:187
  154.8 32.6 %all_gather.45 = bf16[8,4,512]{0,1,2:T(4,128)(2,1)S(1)} all-gather(bf16[8,4,32]{0,1,2:T(4,128)(2,1)} %copy.123), channel_id=1, replica_groups=mesh['group'=16,'tp'=16] {'tp'}, dimensions={2}, use_global_device_ids=true | all-gather | bytes 34816 | tf_op jit(solution)/shard_map/all_gather | solution.py:188
  191.0 1.7 fusion.23
  192.9 34.5 %all_gather.51 = bf16[8,4,512]{0,1,2:T(4,128)(2,1)S(1)} all-gather(bf16[8,4,32]{0,1,2:T(4,128)(2,1)S(1)} %copy.133), channel_id=1, replica_groups=mesh['group'=16,'tp'=16] {'tp'}, dimensions={2}, use_global_device_ids=true | all-gather | bytes 34816 | tf_op jit(solution)/shard_map/all_gather | solution.py:189
  230.7 19.0 %all-gather.6 = bf16[16,4,320]{2,1,0:T(4,128)(2,1)S(1)} all-gather(bf16[1,4,320]{2,1,0:T(4,128)(2,1)S(1)} %bitcast.137), channel_id=1, replica_groups=mesh['group'=16,'tp'=16] {'group'}, dimensions={0}, use_global_device_ids=true | all-gather | bytes 43520 | tf_op jit(solution)/shard_map/all_gather | solution.py:163
  249.7 43.3 %all-gather.7 = bf16[16,320,64]{1,2,0:T(8,128)(2,1)S(1)} all-gather(bf16[1,320,64]{1,2,0:T(8,128)(2,1)S(1)} %bitcast.131), channel_id=1, replica_groups=mesh['group'=16,'tp'=16] {'tp'}, dimensions={0}, use_global_device_ids=true | all-gather | bytes 696320 | tf_op jit(solution)/shard_map/all_gather | solution.py:167
  294.2 21.9 %all-gather.5 = bf16[16,4,256]{2,1,0:T(4,128)(2,1)S(1)} all-gather(bf16[1,4,256]{2,1,0:T(4,128)(2,1)S(1)} %bitcast.139), channel_id=1, replica_groups=mesh['group'=16,'tp'=16] {'group'}, dimensions={0}, use_global_device_ids=true | all-gather | bytes 34816 | tf_op jit(solution)/shard_map/all_gather | solution.py:162
  316.7 33.8 %all_gather.49 = f32[16,8,4,32]{3,1,2,0:T(8,128)S(1)} all-gather(f32[1,8,4,32]{3,1,2,0:T(8,128)S(1)} %all_gather_reshape.10), channel_id=1, replica_groups=mesh['group'=16,'tp'=16] {'tp'}, dimensions={0}, use_global_device_ids=true | all-gather | bytes 69632 | tf_op jit(solution)/shard_map/all_gather | solution.py:14
  350.7 31.2 %all_gather.48 = f32[16,8,4,32]{3,1,2,0:T(8,128)S(1)} all-gather(f32[1,8,4,32]{3,1,2,0:T(8,128)S(1)} %all_gather_reshape.9), channel_id=1, replica_groups=mesh['group'=16,'tp'=16] {'tp'}, dimensions={0}, use_global_device_ids=true | all-gather | bytes 69632 | tf_op jit(solution)/shard_map/all_gather | solution.py:14
  382.0 8.0 %slice.64 = f32[15,8,4,32,128]{4,3,2,1,0:T(8,128)} slice(f32[16,8,4,32,128]{4,3,2,1,0:T(8,128)} %all-gather.11.cloned.1.call-done), slice={[1:16], [0:8], [0:4], [0:32], [0:128]} | slice | bytes 15728640 | tf_op jit(solution)/shard_map/slice | solution.py:16
  391.1 24.2 %while.14 = (s32[]{:T(128)}, f32[8,4,32]{2,1,0:T(4,128)S(1)}, f32[8,4,32]{2,1,0:T(4,128)S(1)}, f32[8,4,32,128]{3,2,1,0:T(8,128)S(1)}, f32[15,8,4,32]{3,1,2,0:T(8...) while((s32[]{:T(128)}, f32[8,4,32]{2,1,0:T(4,128)S(1)}, ...), condition=%wide.region_6.7_spmd, body=%wide.region_5.6_spmd.sunk | while | flops 399362 | bytes 1630301 | solution.py:17
  391.2 1.5 fusion.61
  392.8 1.5 fusion.61
  394.4 1.5 fusion.61
  396.0 1.5 fusion.61
  399.3 1.5 fusion.61
  410.6 1.5 fusion.61
  413.8 1.5 fusion.61
  415.5 3.0 convolution_convert_fusion
  418.5 5.0 copy.150
  423.5 7.2 %reshape.212 = bf16[5120,32]{1,0:T(8,128)(2,1)} reshape(bf16[5120,4,8]{2,1,0:T(4,128)(2,1)} %bitcast.119) | data formatting | bytes 655360
  430.7 66.9 %reduce-scatter.4.cloned.1.call-done = bf16[320,32]{1,0:T(8,128)(2,1)} async-done(((bf16[5120,32]{1,0:T(8,128)(2,1)}), bf16[320,32]{1,0:T(8,128)(2,1)}) %reduce-scatter.4.cloned.1.call-update) | async-done | bytes 20496
  (147 shorter events, 31.5 us)
Async XLA Ops:
  6.5 100.4 %all-gather.13.cloned.1.call-start = ((), (), s32[]{:S(2)}) async-start(), calls=%async_computation.2 | async-start | bytes 2785280 | tf_op jit(solution)/shard_map/all_gather | solution.py:166
  29.4 352.6 %all-gather.11.cloned.1.call-start = ((), (), s32[]{:S(2)}) async-start(), calls=%async_computation.1 | async-start | bytes 8912896 | tf_op jit(solution)/shard_map/all_gather | solution.py:14
  29.4 3.1 copy-start.11
  29.4 25.8 %copy-start.9 = (bf16[5120]{0:T(1024)(128)(2,1)S(1)}, bf16[5120]{0:T(1024)(128)(2,1)}, u32[]{:S(2)}) copy-start(bf16[5120]{0:T(1024)(128)(2,1)} %param.20) | copy-start | bytes 30724
  29.4 25.8 %copy-start.18 = (bf16[128]{0:T(256)(128)(2,1)S(1)}, bf16[128]{0:T(256)(128)(2,1)}, u32[]{:S(2)}) copy-start(bf16[128]{0:T(256)(128)(2,1)} %param.21) | copy-start | bytes 772
  29.4 25.9 %copy-start.2 = (bf16[8,4,5120]{2,1,0:T(4,128)(2,1)S(1)}, bf16[8,4,5120]{2,1,0:T(4,128)(2,1)}, u32[]{:S(2)}) copy-start(bf16[8,4,5120]{2,1,0:T(4,128)(2,1)} %param.19) | copy-start | bytes 983044
  29.5 27.1 %copy-start.19 = (bf16[128]{0:T(256)(128)(2,1)S(1)}, bf16[128]{0:T(256)(128)(2,1)}, u32[]{:S(2)}) copy-start(bf16[128]{0:T(256)(128)(2,1)} %param.22) | copy-start | bytes 772
  55.3 98.3 %copy-start.8 = (f32[5120]{0:T(1024)}, f32[5120]{0:T(1024)S(1)}, u32[]{:S(2)}) copy-start(f32[5120]{0:T(1024)S(1)} %convert_element_type.77) | copy-start | bytes 61444
  56.5 97.1 %copy-start.16 = (f32[32]{0:T(128)}, f32[32]{0:T(128)S(1)}, u32[]{:S(2)}) copy-start(f32[32]{0:T(128)S(1)} %rsqrt.29) | copy-start | bytes 388
  59.4 5.2 %copy-start.14 = (bf16[4,32]{1,0:T(4,128)(2,1)S(1)}, bf16[4,32]{1,0:T(4,128)(2,1)}, u32[]{:S(2)}) copy-start(bf16[4,32]{1,0:T(4,128)(2,1)} %param.29) | copy-start | bytes 772
  59.4 24.4 %copy-start.15 = (bf16[4,32]{1,0:T(4,128)(2,1)S(1)}, bf16[4,32]{1,0:T(4,128)(2,1)}, u32[]{:S(2)}) copy-start(bf16[4,32]{1,0:T(4,128)(2,1)} %param.30) | copy-start | bytes 772
  59.4 46.5 %copy-start.13 = (s32[8]{0:T(128)S(1)}, s32[8]{0:T(128)}, u32[]{:S(2)}) copy-start(s32[8]{0:T(128)} %param.35) | copy-start | bytes 100
  106.9 7.3 %copy-start.6 = (f32[8,4,64]{2,1,0:T(4,128)}, f32[8,4,64]{2,1,0:T(4,128)S(1)}, u32[]{:S(2)}) copy-start(f32[8,4,64]{2,1,0:T(4,128)S(1)} %get-tuple-element.98) | copy-start | bytes 24580
  112.9 40.7 %copy-start.1 = (bf16[192,5120]{1,0:T(8,128)(2,1)S(1)}, bf16[192,5120]{1,0:T(8,128)(2,1)}, u32[]{:S(2)}) copy-start(bf16[192,5120]{1,0:T(8,128)(2,1)} %reshape.194) | copy-start | bytes 5898244
  112.9 40.7 %copy-start.4 = (f32[32,5120]{1,0:T(8,128)S(1)}, f32[32,5120]{1,0:T(8,128)}, u32[]{:S(2)}) copy-start(f32[32,5120]{1,0:T(8,128)} %reshape.182) | copy-start | bytes 1966084
  112.9 40.7 %copy-start.17 = (bf16[5120,32]{0,1:T(8,128)(2,1)S(1)}, bf16[5120,32]{0,1:T(8,128)(2,1)}, u32[]{:S(2)}) copy-start(bf16[5120,32]{0,1:T(8,128)(2,1)} %param.24) | copy-start | bytes 983044
  154.1 73.5 %copy-start = (bf16[8,128,512]{2,0,1:T(8,128)(2,1)S(1)}, bf16[8,128,512]{2,0,1:T(8,128)(2,1)}, u32[]{:S(2)}) copy-start(bf16[8,128,512]{2,0,1:T(8,128)(2,1)} %copy.134) | copy-start | bytes 3145732
  191.0 36.8 %copy-start.5 = (bf16[8,4,4096]{2,0,1:T(8,128)(2,1)S(1)}, bf16[8,4,4096]{2,0,1:T(8,128)(2,1)}, u32[]{:S(2)}) copy-start(bf16[8,4,4096]{2,0,1:T(8,128)(2,1)} %all_gather.47) | copy-start | bytes 786436
  191.0 36.8 %copy-start.7 = (pred[8,4,132]{2,1,0:T(4,128)(4,1)S(1)}, pred[8,4,132]{2,1,0:T(4,128)(4,1)}, u32[]{:S(2)}) copy-start(pred[8,4,132]{2,1,0:T(4,128)(4,1)} %broadcast_select_fusion) | copy-start | bytes 12676
  192.7 35.0 %copy-start.3 = (bf16[8,128,4,128]{3,1,2,0:T(8,128)(2,1)S(1)}, bf16[8,128,4,128]{3,1,2,0:T(8,128)(2,1)}, u32[]{:S(2)}) copy-start(bf16[8,128,4,128]{3,1,2,0:T(8,128)(2,1)} %copy.127) | copy-start | bytes 3145732
  228.8 2.0 copy-start.10
  229.7 64.4 %copy-start.12 = (bf16[256,4]{0,1:T(4,128)(2,1)S(1)}, bf16[256,4]{0,1:T(4,128)(2,1)}, u32[]{:S(2)}) copy-start(bf16[256,4]{0,1:T(4,128)(2,1)} %param.31) | copy-start | bytes 6148
  230.7 267.0 %reduce-scatter.4.cloned.1.call-start = ((), (), s32[]{:S(2)}) async-start(), calls=%async_computation.3 | async-start | bytes 1392640
Sparse Core Ops, SparseCore 0:
  29.5 74.5 all-gather.12
  230.8 104.1 all-gather.10
  430.9 66.7 reduce-scatter.3
where the time goes:
time: 508 us; the launch traced here: 506 us
  blocking collectives  341 us (67%)
  waiting for transfers between devices  67 us (13%)
  local copies, waits for them, and re-layouts  45.1 us (9%)
  other arithmetic  28.2 us (6%)
  between operations  13.6 us (3%)
  matrix products  10.2 us (2%)
    unnamed x4, waiting for transfers between devices  66.9 us
    all_gather x2, blocking collectives, merged(): pieces = jax.tree.map(lambda part: lax.all_gather(part, axis), value)  65 us
    all_gather x1, blocking collectives, local(): lax.all_gather(lift_rows, 'tp', axis=1, tiled=True)  43.3 us
    all_gather x1, blocking collectives, local(): lax.all_gather(queries, 'tp', axis=2, tiled=True)  39.2 us
    all_gather x1, blocking collectives, local(): lax.all_gather(new_values, 'tp', axis=2, tiled=True)  34.5 us
    all_gather x1, blocking collectives, local(): lax.all_gather(raw_keys, 'tp', axis=2, tiled=True)  32.6 us
    unnamed x52, local copies, waits for them, and re-layouts  27 us
    add x15, other arithmetic, blend(): weighted_a * factor_a[..., None] + weighted_b * factor_b[..., None]  23.1 us
  transfers between devices with their start and end apart: 3, of which 1 were waited for; matrix products, arithmetic and copies ran while one was open for 3% of the time, Pallas kernels for 0%

commit v1 on v0

v1 whole, which is shorter than its diff:
```python
import functools
import math

import jax
import jax.numpy as jnp
import numpy as np
from jax import lax
from jax.experimental import pallas as pl
from jax.experimental.pallas import tpu as pltpu
from jax.sharding import PartitionSpec as P

EPS = 1e-06
ADAPTER_SCALE = 2.0
THETA = 1000000.0
PARTS = 16
HEAD = 128
TOKENS = 4
ROWS = 8
F32 = jnp.float32
BF16 = jnp.bfloat16


def call(body, out_shapes, *args, smem=(), flops=0, moved=0):
    specs = [
        pl.BlockSpec(memory_space=pltpu.SMEM if i in smem else pltpu.VMEM)
        for i in range(len(args))
    ]
    return pl.pallas_call(
        body,
        out_shape=out_shapes,
        in_specs=specs,
        out_specs=jax.tree.map(lambda _: pl.BlockSpec(memory_space=pltpu.VMEM), out_shapes),
        compiler_params=pltpu.CompilerParams(vmem_limit_bytes=24 * 2**20),
        cost_estimate=pl.CostEstimate(flops=flops, bytes_accessed=moved, transcendentals=0),
    )(*args)


def dot(a, b, contract=(1, 0)):
    return lax.dot_general(
        a, b, (((contract[0],), (contract[1],)), ((), ())), preferred_element_type=F32
    )


def widen(block, lanes):
    return jnp.concatenate(
        [block, jnp.zeros((block.shape[0], lanes - block.shape[1]), block.dtype)], axis=1
    )


def pack_body(down, out_down, query_up, key_up, value_up, out_up, packed):
    f = lambda ref: ref[...].astype(F32)
    up = jnp.concatenate([f(query_up), f(key_up), f(value_up)], axis=1)
    block = jnp.concatenate(
        [widen(f(down), 384), widen(f(out_down), 384), widen(up, 384), widen(f(out_up), 384)],
        axis=0,
    ).astype(BF16)
    for i in range(PARTS):
        packed[i] = block


def project_body(x_ref, gain, query_w, key_w, value_w, packed, low, base, ups, out_down, out_up):
    x = x_ref[...].astype(F32)
    scale = lax.rsqrt(jnp.mean(x * x, axis=-1, keepdims=True) + EPS)
    normed = (x * scale * gain[...].astype(F32)).astype(BF16)
    pieces = [packed[i].astype(F32) for i in range(PARTS)]
    down = jnp.concatenate([p[0:16, 0:320] for p in pieces], axis=1).astype(BF16)
    low_here = dot(normed, down, (1, 1))
    lane = lax.broadcasted_iota(jnp.int32, low_here.shape, 1)
    low_here = jnp.where(lane < 12, low_here, 0.0)
    block = widen(low_here, 128).astype(BF16)
    for i in range(PARTS):
        low[i] = block
    base[:, 0:256] = dot(normed, query_w[...])
    both = jnp.concatenate([key_w[...], value_w[...]], axis=0)
    base[:, 256:384] = widen(dot(normed, both, (1, 1)), 128)
    out_down[...] = jnp.concatenate([p[12:16, 0:256] for p in pieces], axis=0).astype(BF16)
    ups[...] = jnp.concatenate([p[16:20] for p in pieces], axis=0).astype(BF16)
    out_up[...] = jnp.concatenate([p[20:24] for p in pieces], axis=0).astype(BF16)


def rms_rope(heads, gain, cosines, sines):
    scale = lax.rsqrt(jnp.mean(heads * heads, axis=-1, keepdims=True) + EPS)
    heads = heads * scale * gain
    return heads * cosines + pltpu.roll(heads, 64, 1) * sines


def regroup(count_from, count_to):
    row = lax.broadcasted_iota(jnp.int32, (64, 64), 0)
    col = lax.broadcasted_iota(jnp.int32, (64, 64), 1)
    source = ((row // TOKENS) % count_to) * (count_from * TOKENS)
    source = source + (row // (TOKENS * count_to)) * TOKENS + row % TOKENS
    return jnp.where(col == source, 1.0, 0.0).astype(BF16)


def query_body(low, base, ups, cosines, sines, gain, packed):
    first = jnp.zeros((32, 128), F32)
    second = jnp.zeros((32, 128), F32)
    lane = lax.broadcasted_iota(jnp.int32, (32, 128), 1)
    for t in range(PARTS):
        start = 12 * t
        piece = low[t].astype(F32)
        piece = pltpu.roll(piece, start % 128, 1) if start % 128 else piece
        if start + 12 <= 128:
            first = first + piece
        elif start >= 128:
            second = second + piece
        else:
            first = first + jnp.where(lane >= start, piece, 0.0)
            second = second + jnp.where(lane < start, piece, 0.0)
    lift = ups[...]
    column = lax.broadcasted_iota(jnp.int32, lift.shape, 1)
    zero = jnp.zeros_like(lift)
    lift_query = jnp.where(column < 256, lift, zero)
    lift_key = jnp.where((column >= 256) & (column < 288), lift, zero)
    lift_value = jnp.where((column >= 288) & (column < 320), lift, zero)
    update = dot(first.astype(BF16), jnp.concatenate([lift_query, lift_key], axis=0))
    update = update + dot(
        second.astype(BF16), jnp.concatenate([lift_value, jnp.zeros_like(lift_value)], axis=0)
    )
    raw = base[...] + ADAPTER_SCALE * update
    heads = [
        rms_rope(raw[:, j * HEAD : (j + 1) * HEAD], gain[...], cosines[...], sines[...])
        for j in range(2)
    ]
    queries = jnp.concatenate(heads, axis=0).astype(BF16)
    queries = dot(regroup(8, 2), queries).astype(BF16)
    fresh = raw[:, 256:384]
    fold = jnp.where(lane[0:16] < 64, fresh[0:16], pltpu.roll(fresh[16:32], 64, 1))
    block = jnp.concatenate([queries, fold.astype(BF16)], axis=0)
    for i in range(PARTS):
        packed[i] = block


def softmax_parts(scores, usable):
    masked = jnp.where(usable, scores, -1e30)
    highest = jnp.max(masked, axis=-1, keepdims=True).astype(BF16).astype(F32)
    weights = jnp.where(usable, jnp.exp(masked - highest), 0.0).astype(BF16)
    total = jnp.sum(weights.astype(F32), axis=-1, keepdims=True)
    return highest, weights, total


def attend_body(
    me, lengths, gathered, keys, values, cosines, sines, gain, packed, own_weighted, own_stats
):
    mine = me[0]
    offset = mine * 128
    scaling = 1.0 / math.sqrt(HEAD)
    everything = [gathered[t, 0:64].astype(F32) for t in range(PARTS)]
    lane = lax.broadcasted_iota(jnp.int32, (128, 128), 1)
    stats = jnp.zeros((128, 128), F32)
    held = None
    for b in range(ROWS):
        queries = jnp.concatenate(
            [everything[t][b * 8 : (b + 1) * 8] for t in range(PARTS)], axis=0
        ).astype(BF16)
        scores = jnp.concatenate(
            [
                dot(queries[n * 32 : (n + 1) * 32], keys[b, :, n * HEAD : (n + 1) * HEAD], (1, 1))
                for n in range(4)
            ],
            axis=0,
        )
        usable = lane + offset < lengths[b]
        highest, weights, total = softmax_parts(scores * scaling, usable)
        total_high = total.astype(BF16).astype(F32)
        stats = jnp.where(lane == b, highest, stats)
        stats = jnp.where(lane == 8 + b, total_high, stats)
        stats = jnp.where(lane == 16 + b, total - total_high, stats)
        weighted = [
            dot(weights[n * 32 : (n + 1) * 32], values[b, :, n * HEAD : (n + 1) * HEAD])
            for n in range(4)
        ]
        if b % 2 == 0:
            held = weighted
            continue
        for t in range(PARTS):
            rows = slice(t % 4 * 8, t % 4 * 8 + 8)
            pair = jnp.concatenate([held[t // 4][rows], weighted[t // 4][rows]], axis=0)
            packed[t, (b - 1) * 8 : (b + 1) * 8] = pair.astype(BF16)
    for t in range(PARTS):
        packed[t, 64:80] = jnp.concatenate(
            [stats[t * 8 : (t + 1) * 8], jnp.zeros((8, 128), F32)], axis=0
        ).astype(BF16)

    first = (mine // 4) * 4
    fresh_key = []
    fresh_value = []
    for q in range(4):
        fold = gathered[first + q, 64:80].astype(F32)
        wide = jnp.concatenate([fold, pltpu.roll(fold, 64, 1)], axis=0)
        fresh_key.append(wide[:, 0:32])
        fresh_value.append(wide[:, 32:64])
    new_keys = jnp.concatenate(fresh_key, axis=1).astype(BF16).astype(F32)
    new_keys = rms_rope(new_keys, gain[...], cosines[...], sines[...]).astype(BF16)
    new_values = jnp.concatenate(fresh_value, axis=1).astype(BF16)
    own = gathered[mine, 0:64]
    scores = dot(own, new_keys, (1, 1)) * scaling
    row = lax.broadcasted_iota(jnp.int32, (64, 32), 0)
    col = lax.broadcasted_iota(jnp.int32, (64, 32), 1)
    usable = (row // 8 == col // TOKENS) & (col % TOKENS <= row % TOKENS)
    highest, weights, total = softmax_parts(scores, usable)
    own_weighted[...] = dot(weights, new_values)
    lane = lax.broadcasted_iota(jnp.int32, (8, 128), 1)
    stats = jnp.zeros((8, 128), F32)
    for b in range(ROWS):
        stats = jnp.where(lane == b, highest[b * 8 : (b + 1) * 8], stats)
        stats = jnp.where(lane == 8 + b, total[b * 8 : (b + 1) * 8], stats)
    own_stats[...] = stats


def output_body(gathered, own_weighted, own_stats, output_w, out_down, packed):
    blocks = [gathered[t].astype(F32) for t in range(PARTS)]
    stats = [block[64:72] for block in blocks] + [own_stats[...]]
    values = [block[0:64] for block in blocks] + [own_weighted[...]]
    highest = functools.reduce(jnp.maximum, stats)
    factors = [jnp.exp(jnp.minimum(s - highest, 0.0)) for s in stats]
    total = jnp.zeros((8, 128), F32)
    for s, f in zip(stats, factors):
        total = total + f * (pltpu.roll(s, 120, 1) + pltpu.roll(s, 112, 1))
    lane = lax.broadcasted_iota(jnp.int32, (8, 128), 1)
    inverse = 1.0 / jnp.where(lane < 8, total, 1.0)
    pieces = []
    for b in range(ROWS):
        piece = jnp.zeros((8, 128), F32)
        for v, f in zip(values, factors):
            piece = piece + f[:, b : b + 1] * v[b * 8 : (b + 1) * 8]
        pieces.append(piece * inverse[:, b : b + 1])
    heads = jnp.concatenate(pieces, axis=0).astype(BF16)
    heads = dot(regroup(2, 8), heads).astype(BF16)
    heads = jnp.concatenate([heads[0:32], heads[32:64]], axis=1)
    low = dot(heads, out_down[...], (1, 1))
    partial = dot(heads, output_w[...])
    for t in range(PARTS):
        packed[t] = jnp.concatenate([partial[:, t * 320 : (t + 1) * 320], low], axis=1).astype(
            BF16
        )


def finish_body(gathered, out_up, result):
    total = gathered[0].astype(F32)
    for t in range(1, PARTS):
        total = total + gathered[t].astype(F32)
    update = dot(total[:, 320:384].astype(BF16), out_up[...])
    out = total[:, 0:320] + ADAPTER_SCALE * update[:, 0:320]
    result[...] = out.astype(BF16)


def swap(block, axis):
    return lax.all_to_all(block, axis, 0, 0)


def local(
    layer_inputs,
    input_norm_gain,
    query_norm_gain,
    key_norm_gain,
    query_matrix,
    key_matrix,
    value_matrix,
    output_matrix,
    adapter_down,
    query_up_factor,
    key_up_factor,
    value_up_factor,
    output_down_factor,
    output_up_factor,
    stored_keys,
    stored_values,
    filled_lengths,
):
    shape = jax.ShapeDtypeStruct
    packed = call(
        pack_body,
        shape((PARTS, 24, 384), BF16),
        adapter_down.T,
        output_down_factor.T,
        query_up_factor,
        key_up_factor,
        value_up_factor,
        output_up_factor,
    )
    packed = swap(packed, "group")
    low, base, ups, out_down, out_up = call(
        project_body,
        (
            shape((PARTS, 32, 128), BF16),
            shape((32, 384), F32),
            shape((64, 384), BF16),
            shape((64, 256), BF16),
            shape((64, 384), BF16),
        ),
        layer_inputs.reshape(ROWS * TOKENS, -1),
        input_norm_gain.reshape(1, -1),
        query_matrix,
        key_matrix.T,
        value_matrix.T,
        packed,
    )
    low = swap(low, "tp")
    inverse = THETA ** (-(np.arange(64, dtype=np.float64) * 2.0 / HEAD))
    positions = filled_lengths[:, None] + jnp.arange(TOKENS, dtype=jnp.int32)[None, :]
    angles = positions.astype(F32).reshape(-1, 1) * jnp.asarray(inverse, F32)
    cosines = jnp.cos(angles)
    sines = jnp.sin(angles)
    cosines = jnp.concatenate([cosines, cosines], axis=1)
    sines = jnp.concatenate([-sines, sines], axis=1)
    queries = call(
        query_body,
        shape((PARTS, 80, 128), BF16),
        low,
        base,
        ups,
        cosines,
        sines,
        query_norm_gain.astype(F32).reshape(1, -1),
    )
    queries = swap(queries, "tp")
    me = lax.axis_index("tp").astype(jnp.int32).reshape(1)
    parts, own_weighted, own_stats = call(
        attend_body,
        (shape((PARTS, 80, 128), BF16), shape((64, 128), F32), shape((8, 128), F32)),
        me,
        filled_lengths,
        queries,
        stored_keys,
        stored_values,
        cosines,
        sines,
        key_norm_gain.astype(F32).reshape(1, -1),
        smem=(0, 1),
    )
    parts = swap(parts, "tp")
    partial = call(
        output_body,
        shape((PARTS, 32, 384), BF16),
        parts,
        own_weighted,
        own_stats,
        output_matrix,
        out_down,
    )
    partial = swap(partial, "tp")
    result = call(finish_body, shape((32, 320), BF16), partial, out_up)
    return result.reshape(ROWS, TOKENS, 320)


def solution(mesh):
    in_specs = (
        P("group", None, None),
        P(),
        P(),
        P(),
        P(None, "tp"),
        P(None, "tp"),
        P(None, "tp"),
        P("tp", None),
        P("group", "tp"),
        P("group", "tp"),
        P("group", "tp"),
        P("group", "tp"),
        P("tp", "group"),
        P("group", "tp"),
        P("group", "tp", None),
        P("group", "tp", None),
        P("group"),
    )
    out_specs = P("group", None, "tp")
    return jax.shard_map(local, mesh=mesh, in_specs=in_specs, out_specs=out_specs, check_vma=False)
```

time: 508 us -> 98.9 us (0.19)
  blocking collectives: 341 us -> 31.7 us
  waiting for transfers between devices: 67 us -> 24 us
  local copies, waits for them, and re-layouts: 45.1 us -> 12.7 us
  other arithmetic: 28.2 us -> 1.62 us
  starting transfers between devices: 0.09 us -> 20.3 us
  between operations: 13.6 us -> 0.09 us
  matrix products: 10.2 us -> 0 us
  Pallas kernels: 0 us -> 7.57 us
    all_gather x12 -> x0, blocking collectives: 341 us -> none  [the longest x2 65 us: merged(): pieces = jax.tree.map(lambda part: lax.all_gather(part, axis), value)]
    unnamed x4 -> x0, waiting for transfers between devices: 66.9 us -> none
    all_to_all x0 -> x2, blocking collectives: none -> 31.7 us  [swap(): return lax.all_to_all(block, axis, 0, 0)]
    all_to_all x0 -> x3, waiting for transfers between devices: none -> 24 us  [swap(): return lax.all_to_all(block, axis, 0, 0)]
    add x31 -> x0, other arithmetic: 23.7 us -> none  [the longest x15 23.1 us: blend(): weighted_a * factor_a[..., None] + weighted_b * factor_b[..., None]]
    all_to_all x0 -> x3, starting transfers between devices: none -> 20.3 us  [swap(): return lax.all_to_all(block, axis, 0, 0)]
    unnamed x52 -> x30, local copies, waits for them, and re-layouts: 27 us -> 10.3 us
    dot_general x7 -> x0, matrix products: 10.2 us -> none  [the longest x1 2.98 us: local(): jnp.dot(heads_out, merged_output, preferred_element_type=jnp.float32)]
  transfers between devices with their start and end apart: 3 -> 3, of which waited for: 1 -> 3; matrix products, arithmetic and copies ran while one was open for 3% -> 4% of each run, Pallas kernels for 0% -> 0%
where the time goes in v1:
time: 98.9 us; the launch traced here: 98 us
  blocking collectives  31.7 us (32%)
  waiting for transfers between devices  24 us (24%)
  starting transfers between devices  20.3 us (21%)
  local copies, waits for them, and re-layouts  12.7 us (13%)
  Pallas kernels  7.57 us (8%)
  other arithmetic  1.62 us (2%)
    all_to_all x2, blocking collectives, swap(): return lax.all_to_all(block, axis, 0, 0)  31.7 us
    all_to_all x3, waiting for transfers between devices, swap(): return lax.all_to_all(block, axis, 0, 0)  24 us
    all_to_all x3, starting transfers between devices, swap(): return lax.all_to_all(block, axis, 0, 0)  20.3 us
    unnamed x30, local copies, waits for them, and re-layouts  10.3 us
    pallas_call x6, Pallas kernels, call(): pl.pallas_call(body, out_shape=out_shapes, in_specs=specs, out_specs=jax....  7.57 us
  transfers between devices with their start and end apart: 3, of which 3 were waited for; matrix products, arithmetic and copies ran while one was open for 4% of the time, Pallas kernels for 0%

profile of v1, /device:TPU:2, one launch (start us, length us, event | category | flops | bytes accessed | tf_op | source)
XLA Modules:
  0.0 98.0 jit_solution(8987608916282279224)
XLA Ops:
  0.0 0.7 copy-done.6
  0.7 0.7 copy-done.7
  1.4 0.7 copy-done.8
  2.1 0.7 copy-done.9
  2.8 0.7 copy-done.11
  3.4 0.7 copy-done.12
  4.1 0.8 shard_map.172
  4.9 7.5 %all-to-all-start = ((bf16[16,24,384]{2,1,0:T(8,128)(2,1)}), bf16[16,24,384]{2,1,0:T(8,128)(2,1)S(1)}, u32[]{:S(2)}, u32[]{:S(2)}) async-start(bf16[16,24,384]{2,1,0:T(8,128)(2,1)} %shard_map.172), calls=%async_computation | async-start | bytes 589824 | tf_op jit(solution)/shard_map/all_to_all | solution.py:249
  12.4 0.7 add_convert_fusion
  13.1 1.0 %reshape.42.x_ref = bf16[32,5120]{1,0:T(8,128)(2,1)S(1)} reshape(bf16[8,4,5120]{2,1,0:T(4,128)(2,1)} %param.18) | data formatting | bytes 655360 | tf_op jit(solution)/shard_map/reshape | solution.py:292
  14.2 0.7 reshape.43.gain
  14.9 0.1 convert_element_type.13
  15.0 0.8 fusion
  15.8 3.8 %all-to-all-done.packed = bf16[16,24,384]{2,1,0:T(8,128)(2,1)S(1)} async-done(((bf16[16,24,384]{2,1,0:T(8,128)(2,1)}), bf16[16,24,384]{2,1,0:T(8,128)(2,1)S(1)}, u32[]{:S(2)}, u32[]{:S(2)}) %all-to-all-start) | async-done | bytes 294944 | tf_op jit(solution)/shard_map/all_to_all | solution.py:249
  19.6 1.7 %copy-done = bf16[5120,256]{1,0:T(8,128)(2,1)S(1)} copy-done((bf16[5120,256]{1,0:T(8,128)(2,1)S(1)}, bf16[5120,256]{1,0:T(8,128)(2,1)}, u32[]{:S(2)}) %copy-start) | copy-done | bytes 2621464
  21.3 1.0 copy-done.4
  22.3 1.0 copy-done.5
  23.3 1.1 %shard_map.173 = (bf16[16,32,128]{2,1,0:T(8,128)(2,1)}, f32[32,384]{1,0:T(8,128)S(1)}, bf16[64,384]{1,0:T(8,128)(2,1)S(1)}, bf16[64,256]{1,0:T(8,128)(2,1)S(1)}, bf16[64,384]{1,0:T(8,128)(2,1)S(1)}) custom-call(bf16[32,5120]{1,0:T(8,128)(2,1)S(1)} %reshape.42.x_ref, bf16[1,5120]{1,0:T(2,128)(2,1)S(1)} %reshape.43.gain, bf16[5120,256]{1,0:T(8,128)(2,1)S(1)} %copy-done, ...), custom_call_target="tpu_custom_call" | custom-call | tf_op jit(solution)/shard_map/pallas_call | solution.py:28
  24.4 8.9 %all-to-all-start.1 = ((bf16[16,32,128]{2,1,0:T(8,128)(2,1)}), bf16[16,32,128]{2,1,0:T(8,128)(2,1)S(1)}, u32[]{:S(2)}, u32[]{:S(2)}) async-start(bf16[16,32,128]{2,1,0:T(8,128)(2,1)} %get-tuple-element.13), calls=%async_computation.1 | async-start | bytes 262144 | tf_op jit(solution)/shard_map/all_to_all | solution.py:249
  33.4 0.1 pad_maximum_fusion
  33.4 8.7 %all-to-all-done.1.low = bf16[16,32,128]{2,1,0:T(8,128)(2,1)S(1)} async-done(((bf16[16,32,128]{2,1,0:T(8,128)(2,1)}), bf16[16,32,128]{2,1,0:T(8,128)(2,1)S(1)}, u32[]{:S(2)}, u32[]{:S(2)}) %all-to-all-start.1) | async-done | bytes 131104 | tf_op jit(solution)/shard_map/all_to_all | solution.py:249
  42.2 1.2 %shard_map.174 = bf16[16,80,128]{2,1,0:T(8,128)(2,1)} custom-call(bf16[16,32,128]{2,1,0:T(8,128)(2,1)S(1)} %all-to-all-done.1.low, f32[32,384]{1,0:T(8,128)S(1)} %get-tuple-element.14.base, bf16[64,384]{1,0:T(8,128)(2,1)S(1)} %get-tuple-element.15.ups, f32[32,128]{1,0:T(8,128)S(1)} %get-tuple-element.24.cosines, f32[32,128]{1,0:T(8,128)S(1)} %get-tuple-element.25.sines, ...), custom_call_target="tpu_custom_call" | custom-call | tf_op jit(solution)/shard_map/pallas_call | solution.py:28
  43.4 3.9 %all-to-all-start.2 = ((bf16[16,80,128]{2,1,0:T(8,128)(2,1)}), bf16[16,80,128]{2,1,0:T(8,128)(2,1)S(1)}, u32[]{:S(2)}, u32[]{:S(2)}) async-start(bf16[16,80,128]{2,1,0:T(8,128)(2,1)} %shard_map.174), calls=%async_computation.2 | async-start | bytes 655360 | tf_op jit(solution)/shard_map/all_to_all | solution.py:249
  47.4 11.4 %all-to-all-done.2.gathered = bf16[16,80,128]{2,1,0:T(8,128)(2,1)S(1)} async-done(((bf16[16,80,128]{2,1,0:T(8,128)(2,1)}), bf16[16,80,128]{2,1,0:T(8,128)(2,1)S(1)}, u32[]{:S(2)}, u32[]{:S(2)}) %all-to-all-start.2) | async-done | bytes 327712 | tf_op jit(solution)/shard_map/all_to_all | solution.py:249
  58.8 1.2 %copy-done.2 = bf16[8,128,512]{2,1,0:T(8,128)(2,1)S(1)} copy-done((bf16[8,128,512]{2,1,0:T(8,128)(2,1)S(1)}, bf16[8,128,512]{2,1,0:T(8,128)(2,1)}, u32[]{:S(2)}) %copy-start.2) | copy-done | bytes 1048600
  60.1 1.2 %copy-done.3 = bf16[8,128,512]{2,1,0:T(8,128)(2,1)S(1)} copy-done((bf16[8,128,512]{2,1,0:T(8,128)(2,1)S(1)}, bf16[8,128,512]{2,1,0:T(8,128)(2,1)}, u32[]{:S(2)}) %copy-start.3) | copy-done | bytes 1048600
  61.3 3.1 %shard_map.175 = (bf16[16,80,128]{2,1,0:T(8,128)(2,1)S(1)}, f32[64,128]{1,0:T(8,128)S(1)}, f32[8,128]{1,0:T(8,128)S(1)}) custom-call(s32[1]{0:T(128)} %bitcast.me, s32[8]{0:T(128)S(1)} %copy-done.10, bf16[16,80,128]{2,1,0:T(8,128)(2,1)S(1)} %all-to-all-done.2.gathered, bf16[8,128,512]{2,1,0:T(8,128)(2,1)S(1)} %copy-done.2, ...), custom_call_target="tpu_custom_call" | custom-call | tf_op jit(solution)/shard_map/pallas_call | solution.py:28
  64.3 15.3 %all_to_all.25.gathered = bf16[16,80,128]{2,1,0:T(8,128)(2,1)S(1)} all-to-all(bf16[16,80,128]{2,1,0:T(8,128)(2,1)S(1)} %get-tuple-element.16), channel_id=1, replica_groups=mesh['group'=16,'tp'=16] {'tp'}, dimensions={0} | all-to-all | bytes 655360 | tf_op jit(solution)/shard_map/all_to_all | solution.py:249
  79.6 1.1 %shard_map.176 = bf16[16,32,384]{2,1,0:T(8,128)(2,1)S(1)} custom-call(bf16[16,80,128]{2,1,0:T(8,128)(2,1)S(1)} %all_to_all.25.gathered, f32[64,128]{1,0:T(8,128)S(1)} %get-tuple-element.17.own_weighted, f32[8,128]{1,0:T(8,128)S(1)} %get-tuple-element.18.own_stats, bf16[256,5120]{1,0:T(8,128)(2,1)S(1)} %copy-done.1, ...), custom_call_target="tpu_custom_call" | custom-call | tf_op jit(solution)/shard_map/pallas_call | solution.py:28
  80.7 16.5 %all_to_all.26.gathered = bf16[16,32,384]{2,1,0:T(8,128)(2,1)S(1)} all-to-all(bf16[16,32,384]{2,1,0:T(8,128)(2,1)S(1)} %shard_map.176), channel_id=1, replica_groups=mesh['group'=16,'tp'=16] {'tp'}, dimensions={0} | all-to-all | bytes 786432 | tf_op jit(solution)/shard_map/all_to_all | solution.py:249
  97.2 0.2 shard_map.177
  97.4 0.6 reshape.48
  (21 shorter events, 0.0 us)
Async XLA Ops:
  0.0 0.7 copy-start.6
  0.7 0.7 copy-start.7
  1.4 0.7 copy-start.8
  2.1 0.7 copy-start.9
  2.8 0.7 copy-start.11
  3.4 0.7 copy-start.12
  4.9 14.7 %all-to-all-start = ((bf16[16,24,384]{2,1,0:T(8,128)(2,1)}), bf16[16,24,384]{2,1,0:T(8,128)(2,1)S(1)}, u32[]{:S(2)}, u32[]{:S(2)}) async-start(bf16[16,24,384]{2,1,0:T(8,128)(2,1)} %shard_map.172), calls=%async_computation | async-start | bytes 589824 | tf_op jit(solution)/shard_map/all_to_all | solution.py:249
  12.4 21.1 %copy-start.13 = (bf16[128]{0:T(256)(128)(2,1)S(1)}, bf16[128]{0:T(256)(128)(2,1)}, u32[]{:S(2)}) copy-start(bf16[128]{0:T(256)(128)(2,1)} %param.20) | copy-start | bytes 772
  19.6 1.7 %copy-start = (bf16[5120,256]{1,0:T(8,128)(2,1)S(1)}, bf16[5120,256]{1,0:T(8,128)(2,1)}, u32[]{:S(2)}) copy-start(bf16[5120,256]{1,0:T(8,128)(2,1)} %query_w.1) | copy-start | bytes 7864324
  21.3 1.0 copy-start.4
  22.3 1.0 copy-start.5
  23.2 24.1 %copy-start.14 = (bf16[128]{0:T(256)(128)(2,1)S(1)}, bf16[128]{0:T(256)(128)(2,1)}, u32[]{:S(2)}) copy-start(bf16[128]{0:T(256)(128)(2,1)} %param.21) | copy-start | bytes 772
  23.3 35.6 %copy-start.10 = (s32[8]{0:T(128)S(1)}, s32[8]{0:T(128)}, u32[]{:S(2)}) copy-start(s32[8]{0:T(128)} %lengths.1) | copy-start | bytes 100
  24.4 55.2 %copy-start.1 = (bf16[256,5120]{1,0:T(8,128)(2,1)S(1)}, bf16[256,5120]{1,0:T(8,128)(2,1)}, u32[]{:S(2)}) copy-start(bf16[256,5120]{1,0:T(8,128)(2,1)} %output_w.1) | copy-start | bytes 7864324
  24.4 17.8 %all-to-all-start.1 = ((bf16[16,32,128]{2,1,0:T(8,128)(2,1)}), bf16[16,32,128]{2,1,0:T(8,128)(2,1)S(1)}, u32[]{:S(2)}, u32[]{:S(2)}) async-start(bf16[16,32,128]{2,1,0:T(8,128)(2,1)} %get-tuple-element.13), calls=%async_computation.1 | async-start | bytes 262144 | tf_op jit(solution)/shard_map/all_to_all | solution.py:249
  43.4 15.4 %all-to-all-start.2 = ((bf16[16,80,128]{2,1,0:T(8,128)(2,1)}), bf16[16,80,128]{2,1,0:T(8,128)(2,1)S(1)}, u32[]{:S(2)}, u32[]{:S(2)}) async-start(bf16[16,80,128]{2,1,0:T(8,128)(2,1)} %shard_map.174), calls=%async_computation.2 | async-start | bytes 655360 | tf_op jit(solution)/shard_map/all_to_all | solution.py:249
  58.8 1.2 %copy-start.2 = (bf16[8,128,512]{2,1,0:T(8,128)(2,1)S(1)}, bf16[8,128,512]{2,1,0:T(8,128)(2,1)}, u32[]{:S(2)}) copy-start(bf16[8,128,512]{2,1,0:T(8,128)(2,1)} %keys.1) | copy-start | bytes 3145732
  60.1 1.2 %copy-start.3 = (bf16[8,128,512]{2,1,0:T(8,128)(2,1)S(1)}, bf16[8,128,512]{2,1,0:T(8,128)(2,1)}, u32[]{:S(2)}) copy-start(bf16[8,128,512]{2,1,0:T(8,128)(2,1)} %values.1) | copy-start | bytes 3145732

commit v2 on v1

v2 whole, which is shorter than its diff:
```python
import functools
import math

import jax
import jax.numpy as jnp
import numpy as np
from jax import lax
from jax.experimental import pallas as pl
from jax.experimental.pallas import tpu as pltpu
from jax.sharding import Mesh
from jax.sharding import PartitionSpec as P

EPS = 1e-06
ADAPTER_SCALE = 2.0
THETA = 1000000.0
GROUPS = 16
PARTS = 16
TP = ("far", "near")
HEAD = 128
TOKENS = 4
ROWS = 8
F32 = jnp.float32
BF16 = jnp.bfloat16
SHAPE = jax.ShapeDtypeStruct
WINDOW = 16 * 2**20


def call(body, out_shapes, args, spaces, room, scratch=(), left=(), moved=0):
    places = {"s": pltpu.SMEM, "a": pltpu.HBM, "v": pltpu.VMEM}
    specs = [pl.BlockSpec(memory_space=places[c]) for c in spaces]
    many = isinstance(out_shapes, tuple)
    outs = [
        pl.BlockSpec(memory_space=pltpu.HBM if i in left else pltpu.VMEM)
        for i in range(len(out_shapes) if many else 1)
    ]
    return pl.pallas_call(
        body,
        out_shape=out_shapes,
        in_specs=specs,
        out_specs=tuple(outs) if many else outs[0],
        scratch_shapes=list(scratch),
        compiler_params=pltpu.CompilerParams(vmem_limit_bytes=int((64 - room) * 2**20)),
        cost_estimate=pl.CostEstimate(flops=0, bytes_accessed=moved, transcendentals=0),
    )(*args)


def dot(a, b, contract=(1, 0)):
    return lax.dot_general(
        a, b, (((contract[0],), (contract[1],)), ((), ())), preferred_element_type=F32
    )


def widen(block, lanes):
    return jnp.concatenate(
        [block, jnp.zeros((block.shape[0], lanes - block.shape[1]), block.dtype)], axis=1
    )


def iotas(shape):
    return [lax.broadcasted_iota(jnp.int32, shape, d) for d in range(2)]


def fetch(sources, held, sems):
    copies = [pltpu.make_async_copy(s, h, sems.at[i]) for i, (s, h) in enumerate(zip(sources, held))]
    for copy in copies:
        copy.start()
    return copies


def pack_body(*refs):
    packed, held = refs[6], refs[7:13]
    for copy in fetch(refs[:6], held, refs[13]):
        copy.wait()
    down, out_down, query_up, key_up, value_up, out_up = [h[...].astype(F32) for h in held]
    up = jnp.concatenate([query_up, key_up, value_up], axis=1)
    block = jnp.concatenate(
        [widen(down, 384), widen(out_down, 384), widen(up, 384), widen(out_up, 384)], axis=0
    ).astype(BF16)
    for i in range(GROUPS):
        packed[i] = block


def normed_body(
    lengths, x_any, gain_any, inverse_any, normed, cosines, sines, x_ref, gain, inverse, sems
):
    for copy in fetch((x_any, gain_any, inverse_any), (x_ref, gain, inverse), sems):
        copy.wait()
    x = x_ref[...].astype(F32).reshape(ROWS * TOKENS, -1)
    scale = lax.rsqrt(jnp.mean(x * x, axis=-1, keepdims=True) + EPS)
    normed[...] = (x * scale * gain[...].astype(F32).reshape(1, -1)).astype(BF16)
    row, lane = iotas((ROWS * TOKENS, HEAD))
    position = row % TOKENS
    for b in range(ROWS):
        position = position + jnp.where(row // TOKENS == b, lengths[b], 0)
    angles = position.astype(F32) * inverse[...]
    cosines[...] = jnp.cos(angles)
    sines[...] = jnp.where(lane < 64, -1.0, 1.0) * jnp.sin(angles)


def low_body(packed, normed, low):
    pieces = [packed[g, 0:16, 0:320].astype(F32) for g in range(GROUPS)]
    down = jnp.concatenate(pieces, axis=1).astype(BF16)
    block = widen(dot(down, normed[...], (1, 1)), 128).astype(BF16)
    for t in range(PARTS):
        low[t] = block


CHUNKS = 4


def base_body(
    packed, normed, query_any, key_any, value_any, base, ups, out_down, out_up,
    query_w, key_w, value_w, sems,
):
    step = query_any.shape[0] // CHUNKS
    rows = [pl.ds(c * step, step) for c in range(CHUNKS)]
    copies = fetch(
        [query_any.at[r] for r in rows] + [key_any, value_any],
        [query_w.at[r] for r in rows] + [key_w, value_w],
        sems,
    )
    pieces = [packed[g].astype(F32) for g in range(GROUPS)]
    out_down[...] = jnp.concatenate([p[12:16, 0:256] for p in pieces], axis=0).astype(BF16)
    ups[...] = jnp.concatenate([p[16:20] for p in pieces], axis=0).astype(BF16)
    out_up[...] = jnp.concatenate([p[20:24] for p in pieces], axis=0).astype(BF16)
    value = normed[...]
    raw = jnp.zeros((32, 256), F32)
    for c in range(CHUNKS):
        copies[c].wait()
        part = slice(c * step, (c + 1) * step)
        raw = raw + dot(value[:, part], query_w[part, :])
    base[:, 0:256] = raw
    copies[CHUNKS].wait()
    copies[CHUNKS + 1].wait()
    both = jnp.concatenate([key_w[...], value_w[...]], axis=0)
    base[:, 256:384] = widen(dot(value, both, (1, 1)), 128)


def rms_rope(heads, gain, cosines, sines):
    scale = lax.rsqrt(jnp.mean(heads * heads, axis=-1, keepdims=True) + EPS)
    heads = heads * scale * gain
    return heads * cosines + pltpu.roll(heads, 64, 1) * sines


def regroup(count_from, count_to):
    row, col = iotas((64, 64))
    source = ((row // TOKENS) % count_to) * (count_from * TOKENS)
    source = source + (row // (TOKENS * count_to)) * TOKENS + row % TOKENS
    return jnp.where(col == source, 1.0, 0.0).astype(BF16)


def query_body(low, base, ups, cosines, sines, gain, packed, own, fresh):
    ranks = jnp.concatenate([low[t].astype(F32)[0:12] for t in range(PARTS)], axis=0)
    ranks = ranks[:, 0:32].astype(BF16)
    lift = ups[...]
    _, column = iotas(lift.shape)
    zero = jnp.zeros_like(lift)
    lifts = [
        jnp.where((column >= first) & (column < last), lift, zero)
        for first, last in ((0, 256), (256, 288), (288, 320))
    ]
    update = dot(ranks, jnp.concatenate(lifts, axis=0), (0, 0))
    raw = base[...] + ADAPTER_SCALE * update
    scale = gain[...].astype(F32).reshape(1, -1)
    heads = [
        rms_rope(raw[:, j * HEAD : (j + 1) * HEAD], scale, cosines[...], sines[...])
        for j in range(2)
    ]
    queries = jnp.concatenate(heads, axis=0).astype(BF16)
    queries = dot(regroup(8, 2), queries).astype(BF16)
    for i in range(PARTS):
        packed[i] = queries
    own[...] = queries
    _, lane = iotas((16, 128))
    folded = jnp.where(lane < 64, raw[0:16, 256:384], pltpu.roll(raw[16:32, 256:384], 64, 1))
    fresh[...] = folded.astype(BF16)


def softmax_parts(scores, usable):
    masked = jnp.where(usable, scores, -1e30)
    highest = jnp.max(masked, axis=-1, keepdims=True).astype(BF16).astype(F32)
    weights = jnp.where(usable, jnp.exp(masked - highest), 0.0).astype(BF16)
    total = jnp.sum(weights.astype(F32), axis=-1, keepdims=True)
    return highest, weights, total


SCALING = 1.0 / math.sqrt(HEAD)
SPAN = 128


def attend_body(place, lengths, gathered, keys, values, packed):
    offset = place[0] * SPAN
    everything = [gathered[t].astype(F32) for t in range(PARTS)]
    _, lane = iotas((128, 128))
    stats = jnp.zeros((128, 128), F32)
    found = []
    for b in range(ROWS):
        query = jnp.concatenate(
            [q[b * 8 : (b + 1) * 8] for q in everything], axis=0
        ).astype(BF16)
        scores = jnp.concatenate(
            [
                dot(query[n * 32 : (n + 1) * 32], keys[b, :, n * HEAD : (n + 1) * HEAD], (1, 1))
                for n in range(4)
            ],
            axis=0,
        )
        highest, weights, total = softmax_parts(scores * SCALING, lane + offset < lengths[b])
        total_high = total.astype(BF16).astype(F32)
        stats = jnp.where(lane == b, highest, stats)
        stats = jnp.where(lane == 8 + b, total_high, stats)
        stats = jnp.where(lane == 16 + b, total - total_high, stats)
        found.append(
            [
                dot(weights[n * 32 : (n + 1) * 32], values[b, :, n * HEAD : (n + 1) * HEAD])
                for n in range(4)
            ]
        )
    for t in range(PARTS):
        rows = slice(t % 4 * 8, t % 4 * 8 + 8)
        block = [found[b][t // 4][rows] for b in range(ROWS)] + [stats[t * 8 : (t + 1) * 8]]
        packed[t] = jnp.concatenate(block, axis=0).astype(BF16)


def fresh_body(
    place, near, near_1, near_2, near_3, own, cosines, sines, gain, weighted, stats_out, gathered
):
    for k, piece in enumerate((near, near_1, near_2, near_3)):
        gathered[(place[0] % 4) ^ k] = piece[...].astype(F32)
    fresh_key = []
    fresh_value = []
    for q in range(4):
        fold = gathered[q]
        wide = jnp.concatenate([fold, pltpu.roll(fold, 64, 1)], axis=0)
        fresh_key.append(wide[:, 0:32])
        fresh_value.append(wide[:, 32:64])
    new_keys = jnp.concatenate(fresh_key, axis=1)
    scale = gain[...].astype(F32).reshape(1, -1)
    new_keys = rms_rope(new_keys, scale, cosines[...], sines[...]).astype(BF16)
    new_values = jnp.concatenate(fresh_value, axis=1).astype(BF16)
    scores = dot(own[...], new_keys, (1, 1)) * SCALING
    row, col = iotas((64, 32))
    usable = (row // 8 == col // TOKENS) & (col % TOKENS <= row % TOKENS)
    highest, weights, total = softmax_parts(scores, usable)
    weighted[...] = dot(weights, new_values)
    _, lane = iotas((8, 128))
    stats = jnp.zeros((8, 128), F32)
    for b in range(ROWS):
        stats = jnp.where(lane == b, highest[b * 8 : (b + 1) * 8], stats)
        stats = jnp.where(lane == 8 + b, total[b * 8 : (b + 1) * 8], stats)
    stats_out[...] = stats


def output_body(
    gathered, own_weighted, own_stats, output_any, out_down, packed, output_w, sems
):
    step = output_any.shape[1] // CHUNKS
    parts = [pl.ds(c * step, step) for c in range(CHUNKS)]
    copies = fetch(
        [output_any.at[:, part] for part in parts], [output_w.at[:, part] for part in parts], sems
    )
    blocks = [gathered[t].astype(F32) for t in range(PARTS)]
    stats = [block[64:72] for block in blocks] + [own_stats[...]]
    values = [block[0:64] for block in blocks] + [own_weighted[...]]
    highest = functools.reduce(jnp.maximum, stats)
    factors = [jnp.exp(jnp.minimum(s - highest, 0.0)) for s in stats]
    total = jnp.zeros((8, 128), F32)
    for s, f in zip(stats, factors):
        total = total + f * (pltpu.roll(s, 120, 1) + pltpu.roll(s, 112, 1))
    _, lane = iotas((8, 128))
    inverse = 1.0 / jnp.where(lane < 8, total, 1.0)
    pieces = []
    for b in range(ROWS):
        piece = jnp.zeros((8, 128), F32)
        for v, f in zip(values, factors):
            piece = piece + f[:, b : b + 1] * v[b * 8 : (b + 1) * 8]
        pieces.append(piece * inverse[:, b : b + 1])
    heads = jnp.concatenate(pieces, axis=0).astype(BF16)
    heads = dot(regroup(2, 8), heads).astype(BF16)
    heads = jnp.concatenate([heads[0:32], heads[32:64]], axis=1)
    low = dot(heads, out_down[...], (1, 1))
    share = PARTS // CHUNKS
    for c in range(CHUNKS):
        copies[c].wait()
        partial = dot(heads, output_w[:, c * step : (c + 1) * step])
        for t in range(share):
            block = jnp.concatenate([partial[:, t * 320 : (t + 1) * 320], low], axis=1)
            packed[c * share + t] = block.astype(BF16)


def finish_body(gathered, out_up, result):
    total = gathered[0].astype(F32)
    for t in range(1, PARTS):
        total = total + gathered[t].astype(F32)
    update = dot(total[:, 320:384].astype(BF16), out_up[...])
    out = total[:, 0:320] + ADAPTER_SCALE * update[:, 0:320]
    result[...] = out.reshape(ROWS, TOKENS, 320).astype(BF16)


def swap(block, axis):
    return lax.all_to_all(block, axis, 0, 0)


def local(
    layer_inputs,
    input_norm_gain,
    query_norm_gain,
    key_norm_gain,
    query_matrix,
    key_matrix,
    value_matrix,
    output_matrix,
    adapter_down,
    query_up_factor,
    key_up_factor,
    value_up_factor,
    output_down_factor,
    output_up_factor,
    stored_keys,
    stored_values,
    filled_lengths,
):
    dma = pltpu.SemaphoreType.DMA
    width = layer_inputs.shape[-1]
    place = lax.axis_index(TP).astype(jnp.int32).reshape(1)
    shards = (
        adapter_down.T,
        output_down_factor.T,
        query_up_factor,
        key_up_factor,
        value_up_factor,
        output_up_factor,
    )
    packed = call(
        pack_body,
        SHAPE((GROUPS, 24, 384), BF16),
        shards,
        "aaaaaa",
        8,
        [pltpu.VMEM(s.shape, BF16) for s in shards] + [dma((6,))],
    )
    packed = swap(packed, "group")

    inverse = THETA ** (-(np.arange(64, dtype=np.float64) * 2.0 / HEAD))
    inverse = jnp.asarray(np.concatenate([inverse, inverse]).reshape(1, HEAD), F32)
    normed, cosines, sines = call(
        normed_body,
        (SHAPE((32, width), BF16), SHAPE((32, HEAD), F32), SHAPE((32, HEAD), F32)),
        (filled_lengths, layer_inputs, input_norm_gain, inverse),
        "saaa",
        12,
        [
            pltpu.VMEM(layer_inputs.shape, BF16),
            pltpu.VMEM((width,), BF16),
            pltpu.VMEM((1, HEAD), F32),
            dma((3,)),
        ],
        moved=WINDOW,
    )
    low = call(low_body, SHAPE((PARTS, 16, 128), BF16), (packed, normed), "vv", 20)
    low = swap(low, TP)
    base, ups, out_down, out_up = call(
        base_body,
        (
            SHAPE((32, 384), F32),
            SHAPE((64, 384), BF16),
            SHAPE((64, 256), BF16),
            SHAPE((64, 384), BF16),
        ),
        (packed, normed, query_matrix, key_matrix.T, value_matrix.T),
        "vvaaa",
        12,
        [
            pltpu.VMEM(query_matrix.shape, BF16),
            pltpu.VMEM((32, width), BF16),
            pltpu.VMEM((32, width), BF16),
            dma((CHUNKS + 2,)),
        ],
        moved=WINDOW,
    )
    queries, own, fresh = call(
        query_body,
        (SHAPE((PARTS, 64, 128), BF16), SHAPE((64, 128), BF16), SHAPE((16, 128), BF16)),
        (low, base, ups, cosines, sines, query_norm_gain),
        "vvvvvv",
        20,
    )
    gathered = swap(queries, TP)
    fresh = [fresh] + [
        lax.ppermute(fresh, "near", [(i, i ^ k) for i in range(4)]) for k in range(1, 4)
    ]
    parts = call(
        attend_body,
        SHAPE((PARTS, 72, 128), BF16),
        (place, filled_lengths, gathered, stored_keys, stored_values),
        "ssvvv",
        20,
    )
    parts = swap(parts, TP)
    own_weighted, own_stats = call(
        fresh_body,
        (SHAPE((64, 128), F32), SHAPE((8, 128), F32)),
        (place, *fresh, own, cosines, sines, key_norm_gain),
        "svvvvvvvv",
        20,
        [pltpu.VMEM((4, 16, 128), F32)],
        moved=WINDOW,
    )
    partial = call(
        output_body,
        SHAPE((PARTS, 32, 384), BF16),
        (parts, own_weighted, own_stats, output_matrix, out_down),
        "vvvav",
        12,
        [pltpu.VMEM(output_matrix.shape, BF16), dma((CHUNKS,))],
    )
    partial = swap(partial, TP)
    return call(finish_body, SHAPE((ROWS, TOKENS, 320), BF16), (partial, out_up), "vv", 20)


def solution(mesh):
    fine = Mesh(mesh.devices.reshape(16, 4, 4), ("group", "far", "near"))
    group, tp = "group", TP
    in_specs = (
        P(group, None, None),
        P(),
        P(),
        P(),
        P(None, tp),
        P(None, tp),
        P(None, tp),
        P(tp, None),
        P(group, tp),
        P(group, tp),
        P(group, tp),
        P(group, tp),
        P(tp, group),
        P(group, tp),
        P(group, tp, None),
        P(group, tp, None),
        P(group),
    )
    out_specs = P(group, None, tp)
    return jax.shard_map(local, mesh=fine, in_specs=in_specs, out_specs=out_specs, check_vma=False)
```

time: 98.9 us -> 90.7 us (0.917)
  blocking collectives: 31.7 us -> 17.6 us
  starting transfers between devices: 20.3 us -> 29.1 us
  local copies, waits for them, and re-layouts: 12.7 us -> 4.94 us
  Pallas kernels: 7.57 us -> 15 us
  other arithmetic: 1.62 us -> 0 us
    all_to_all x2 -> x1, blocking collectives: 31.7 us -> 17.6 us  [swap(): return lax.all_to_all(block, axis, 0, 0)]
    pallas_call x6 -> x9, Pallas kernels: 7.57 us -> 15 us  [call(): pl.pallas_call(body, out_shape=out_shapes, in_specs=specs, out_specs=tupl...]
    all_to_all x3 -> x4, waiting for transfers between devices: 24 us -> 18.6 us  [swap(): return lax.all_to_all(block, axis, 0, 0)]
    unnamed x30 -> x22, local copies, waits for them, and re-layouts: 10.3 us -> 4.94 us
    ppermute x0 -> x3, waiting for transfers between devices: none -> 4.69 us  [local(): lax.ppermute(fresh, 'near', [(i, i ^ k) for i in range(4)])]
    ppermute x0 -> x3, starting transfers between devices: none -> 4.47 us  [local(): lax.ppermute(fresh, 'near', [(i, i ^ k) for i in range(4)])]
    all_to_all x3 -> x4, starting transfers between devices: 20.3 us -> 24.7 us  [swap(): return lax.all_to_all(block, axis, 0, 0)]
    reshape x3 -> x0, local copies, waits for them, and re-layouts: 2.39 us -> none  [the longest x1 1.05 us: local(): layer_inputs.reshape(ROWS * TOKENS, -1)]
  transfers between devices with their start and end apart: 3 -> 7, of which waited for: 3 -> 5; matrix products, arithmetic and copies ran while one was open for 4% -> 0% of each run, Pallas kernels for 0% -> 5%
where the time goes in v2:
time: 90.7 us; the launch traced here: 90 us
  starting transfers between devices  29.1 us (32%)
  waiting for transfers between devices  23.2 us (26%)
  blocking collectives  17.6 us (19%)
  Pallas kernels  15 us (17%)
  local copies, waits for them, and re-layouts  4.94 us (5%)
    all_to_all x4, starting transfers between devices, swap(): return lax.all_to_all(block, axis, 0, 0)  24.7 us
    all_to_all x4, waiting for transfers between devices, swap(): return lax.all_to_all(block, axis, 0, 0)  18.6 us
    all_to_all x1, blocking collectives, swap(): return lax.all_to_all(block, axis, 0, 0)  17.6 us
    pallas_call x9, Pallas kernels, call(): pl.pallas_call(body, out_shape=out_shapes, in_specs=specs, out_specs=tupl...  15 us
    unnamed x22, local copies, waits for them, and re-layouts  4.94 us
    ppermute x3, waiting for transfers between devices, local(): lax.ppermute(fresh, 'near', [(i, i ^ k) for i in range(4)])  4.69 us
    ppermute x3, starting transfers between devices, local(): lax.ppermute(fresh, 'near', [(i, i ^ k) for i in range(4)])  4.47 us
  transfers between devices with their start and end apart: 7, of which 5 were waited for; matrix products, arithmetic and copies ran while one was open for 0% of the time, Pallas kernels for 5%

profile of v2, /device:TPU:2, one launch (start us, length us, event | category | flops | bytes accessed | tf_op | source)
XLA Modules:
  0.0 90.0 jit_solution(16059840581512215705)
XLA Ops:
  0.0 1.6 %shard_map.172 = bf16[16,24,384]{2,1,0:T(8,128)(2,1)} custom-call(bf16[12,320]{1,0:T(8,128)(2,1)} %bitcast.7, bf16[4,256]{1,0:T(4,128)(2,1)} %bitcast.8, bf16[4,256]{1,0:T(4,128)(2,1)} %refs_2_.1, bf16[4,32]{1,0:T(4,128)(2,1)} %refs_3_.1, bf16[4,32]{1,0:T(4,128)(2,1)} %refs_4_.1, bf16[4,320]{1,0:T(4,128)(2,1)} %refs_5_.1), custom_call_target="tpu_custom_call" | custom-call | tf_op jit(solution)/shard_map/pallas_call | solution.py:36
  1.6 7.5 %all-to-all-start = ((bf16[16,24,384]{2,1,0:T(8,128)(2,1)}), bf16[16,24,384]{2,1,0:T(8,128)(2,1)S(1)}, u32[]{:S(2)}, u32[]{:S(2)}) async-start(bf16[16,24,384]{2,1,0:T(8,128)(2,1)} %shard_map.172), calls=%async_computation | async-start | bytes 589824 | tf_op jit(solution)/shard_map/all_to_all | solution.py:301
  9.1 1.0 %copy-done.2 = bf16[8,4,5120]{2,1,0:T(4,128)(2,1)S(1)} copy-done((bf16[8,4,5120]{2,1,0:T(4,128)(2,1)S(1)}, bf16[8,4,5120]{2,1,0:T(4,128)(2,1)}, u32[]{:S(2)}) %copy-start.2) | copy-done | bytes 327704
  10.1 0.7 copy-done.5
  10.8 0.7 copy-done.6
  11.4 0.7 copy-done.10
  12.1 1.0 %shard_map.173 = (bf16[32,5120]{1,0:T(8,128)(2,1)S(1)}, f32[32,128]{1,0:T(8,128)S(1)}, f32[32,128]{1,0:T(8,128)S(1)}) custom-call(s32[8]{0:T(128)S(1)} %copy-done.6, bf16[8,4,5120]{2,1,0:T(4,128)(2,1)S(1)} %copy-done.2, bf16[5120]{0:T(1024)(128)(2,1)S(1)} %copy-done.5, f32[1,128]{1,0:T(1,128)S(1)} %copy-done.10), custom_call_target="tpu_custom_call" | custom-call | bytes 16777216 | tf_op jit(solution)/shard_map/pallas_call | solution.py:36
  13.1 3.2 %all-to-all-done.packed = bf16[16,24,384]{2,1,0:T(8,128)(2,1)S(1)} async-done(((bf16[16,24,384]{2,1,0:T(8,128)(2,1)}), bf16[16,24,384]{2,1,0:T(8,128)(2,1)S(1)}, u32[]{:S(2)}, u32[]{:S(2)}) %all-to-all-start) | async-done | bytes 294944 | tf_op jit(solution)/shard_map/all_to_all | solution.py:301
  16.3 0.9 shard_map.174
  17.2 8.7 %all-to-all-start.1 = ((bf16[16,16,128]{2,1,0:T(8,128)(2,1)}), bf16[16,16,128]{2,1,0:T(8,128)(2,1)S(1)}, u32[]{:S(2)}, u32[]{:S(2)}) async-start(bf16[16,16,128]{2,1,0:T(8,128)(2,1)} %shard_map.174), calls=%async_computation.1 | async-start | bytes 131072 | tf_op jit(solution)/shard_map/all_to_all | solution.py:301
  25.9 0.0 copy-start.3
  25.9 1.0 %copy-done.3 = bf16[5120,32]{0,1:T(8,128)(2,1)S(1)} copy-done((bf16[5120,32]{0,1:T(8,128)(2,1)S(1)}, bf16[5120,32]{0,1:T(8,128)(2,1)}, u32[]{:S(2)}) %copy-start.3) | copy-done | bytes 327704
  26.8 1.0 %copy-done.4 = bf16[5120,32]{0,1:T(8,128)(2,1)S(1)} copy-done((bf16[5120,32]{0,1:T(8,128)(2,1)S(1)}, bf16[5120,32]{0,1:T(8,128)(2,1)}, u32[]{:S(2)}) %copy-start.4) | copy-done | bytes 327704
  27.8 2.6 %shard_map.175 = (f32[32,384]{1,0:T(8,128)S(1)}, bf16[64,384]{1,0:T(8,128)(2,1)S(1)}, bf16[64,256]{1,0:T(8,128)(2,1)S(1)}, bf16[64,384]{1,0:T(8,128)(2,1)S(1)}) custom-call(bf16[16,24,384]{2,1,0:T(8,128)(2,1)S(1)} %all-to-all-done.packed, bf16[32,5120]{1,0:T(8,128)(2,1)S(1)} %get-tuple-element.17.normed, bf16[5120,256]{1,0:T(8,128)(2,1)} %query_any.1, ...), custom_call_target="tpu_custom_call" | custom-call | bytes 16777216 | tf_op jit(solution)/shard_map/pallas_call | solution.py:36
  30.4 0.0 copy-start.9
  30.4 4.1 %all-to-all-done.1.low = bf16[16,16,128]{2,1,0:T(8,128)(2,1)S(1)} async-done(((bf16[16,16,128]{2,1,0:T(8,128)(2,1)}), bf16[16,16,128]{2,1,0:T(8,128)(2,1)S(1)}, u32[]{:S(2)}, u32[]{:S(2)}) %all-to-all-start.1) | async-done | bytes 65568 | tf_op jit(solution)/shard_map/all_to_all | solution.py:301
  34.5 1.2 %shard_map.176 = (bf16[16,64,128]{2,1,0:T(8,128)(2,1)}, bf16[64,128]{1,0:T(8,128)(2,1)S(1)}, bf16[16,128]{1,0:T(8,128)(2,1)S(1)}) custom-call(bf16[16,16,128]{2,1,0:T(8,128)(2,1)S(1)} %all-to-all-done.1.low, f32[32,384]{1,0:T(8,128)S(1)} %get-tuple-element.18.base, bf16[64,384]{1,0:T(8,128)(2,1)S(1)} %get-tuple-element.19.ups, ...), custom_call_target="tpu_custom_call" | custom-call | tf_op jit(solution)/shard_map/pallas_call | solution.py:36
  35.7 4.1 %all-to-all-start.2 = ((bf16[16,64,128]{2,1,0:T(8,128)(2,1)}), bf16[16,64,128]{2,1,0:T(8,128)(2,1)S(1)}, u32[]{:S(2)}, u32[]{:S(2)}) async-start(bf16[16,64,128]{2,1,0:T(8,128)(2,1)} %get-tuple-element.22), calls=%async_computation.2 | async-start | bytes 524288 | tf_op jit(solution)/shard_map/all_to_all | solution.py:301
  39.7 10.5 %all-to-all-done.2.gathered = bf16[16,64,128]{2,1,0:T(8,128)(2,1)S(1)} async-done(((bf16[16,64,128]{2,1,0:T(8,128)(2,1)}), bf16[16,64,128]{2,1,0:T(8,128)(2,1)S(1)}, u32[]{:S(2)}, u32[]{:S(2)}) %all-to-all-start.2) | async-done | bytes 262176 | tf_op jit(solution)/shard_map/all_to_all | solution.py:301
  50.3 3.6 %shard_map.177 = bf16[16,72,128]{2,1,0:T(8,128)(2,1)} custom-call(s32[1]{0:T(128)} %bitcast.place, s32[8]{0:T(128)S(1)} %copy-done.7, bf16[16,64,128]{2,1,0:T(8,128)(2,1)S(1)} %all-to-all-done.2.gathered, bf16[8,128,512]{2,1,0:T(8,128)(2,1)S(1)} %copy-done, bf16[8,128,512]{2,1,0:T(8,128)(2,1)S(1)} %copy-done.1), custom_call_target="tpu_custom_call" | custom-call | tf_op jit(solution)/shard_map/pallas_call | solution.py:36
  53.8 4.4 %all-to-all-start.3 = ((bf16[16,72,128]{2,1,0:T(8,128)(2,1)}), bf16[16,72,128]{2,1,0:T(8,128)(2,1)S(1)}, u32[]{:S(2)}, u32[]{:S(2)}) async-start(bf16[16,72,128]{2,1,0:T(8,128)(2,1)} %shard_map.177), calls=%async_computation.3 | async-start | bytes 589824 | tf_op jit(solution)/shard_map/all_to_all | solution.py:301
  58.3 3.7 %collective-permute-start.2 = (bf16[16,128]{1,0:T(8,128)(2,1)S(1)}, bf16[16,128]{1,0:T(8,128)(2,1)S(1)}, u32[]{:S(2)}, u32[]{:S(2)}) collective-permute-start(bf16[16,128]{1,0:T(8,128)(2,1)S(1)} %get-tuple-element.23.near), channel_id=1, source_target_pairs={{0,3},{1,2},{2,1},{3,0},{4,7},{5,6},{6,5},{7,4},{8,11},{9,10},{10,... | collective-permute-start | bytes 12296 | tf_op jit(solution)/shard_map/ppermute | solution.py:390
  62.0 0.0 collective-permute-start.1
  62.0 0.7 collective-permute-start
  62.8 4.7 %collective-permute-done.2.near_3 = bf16[16,128]{1,0:T(8,128)(2,1)S(1)} collective-permute-done((bf16[16,128]{1,0:T(8,128)(2,1)S(1)}, bf16[16,128]{1,0:T(8,128)(2,1)S(1)}, u32[]{:S(2)}, u32[]{:S(2)}) %collective-permute-start.2) | collective-permute-done | bytes 4128 | tf_op jit(solution)/shard_map/ppermute | solution.py:390
  67.5 0.0 collective-permute-done.1.near_2
  67.5 0.0 collective-permute-done.near_1
  67.5 0.6 shard_map.178
  68.1 0.8 all-to-all-done.3.gathered
  68.9 2.7 %shard_map.179 = bf16[16,32,384]{2,1,0:T(8,128)(2,1)S(1)} custom-call(bf16[16,72,128]{2,1,0:T(8,128)(2,1)S(1)} %all-to-all-done.3.gathered, f32[64,128]{1,0:T(8,128)S(1)} %get-tuple-element.25.own_weighted, f32[8,128]{1,0:T(8,128)S(1)} %get-tuple-element.26.own_stats, bf16[256,5120]{1,0:T(8,128)(2,1)} %output_any.1, ...), custom_call_target="tpu_custom_call" | custom-call | tf_op jit(solution)/shard_map/pallas_call | solution.py:36
  71.6 17.6 %all_to_all.25.gathered = bf16[16,32,384]{2,1,0:T(8,128)(2,1)S(1)} all-to-all(bf16[16,32,384]{2,1,0:T(8,128)(2,1)S(1)} %shard_map.179), channel_id=1, replica_groups=mesh['group'=16,'far'=4,'near'=4] {'far','near'}, dimensions={0} | all-to-all | bytes 786432 | tf_op jit(solution)/shard_map/all_to_all | solution.py:301
  89.1 0.8 shard_map.180
  (14 shorter events, 0.0 us)
Async XLA Ops:
  1.6 14.7 %all-to-all-start = ((bf16[16,24,384]{2,1,0:T(8,128)(2,1)}), bf16[16,24,384]{2,1,0:T(8,128)(2,1)S(1)}, u32[]{:S(2)}, u32[]{:S(2)}) async-start(bf16[16,24,384]{2,1,0:T(8,128)(2,1)} %shard_map.172), calls=%async_computation | async-start | bytes 589824 | tf_op jit(solution)/shard_map/all_to_all | solution.py:301
  9.1 1.0 %copy-start.2 = (bf16[8,4,5120]{2,1,0:T(4,128)(2,1)S(1)}, bf16[8,4,5120]{2,1,0:T(4,128)(2,1)}, u32[]{:S(2)}) copy-start(bf16[8,4,5120]{2,1,0:T(4,128)(2,1)} %x_any.1) | copy-start | bytes 983044
  10.1 0.7 copy-start.5
  10.8 0.7 copy-start.6
  11.4 0.7 copy-start.10
  12.1 22.4 %copy-start.8 = (bf16[128]{0:T(256)(128)(2,1)S(1)}, bf16[128]{0:T(256)(128)(2,1)}, u32[]{:S(2)}) copy-start(bf16[128]{0:T(256)(128)(2,1)} %gain.2) | copy-start | bytes 772
  16.3 34.0 %copy-start.7 = (s32[8]{0:T(128)S(1)}, s32[8]{0:T(128)}, u32[]{:S(2)}) copy-start(s32[8]{0:T(128)} %lengths.3) | copy-start | bytes 100
  16.3 34.0 %copy-start = (bf16[8,128,512]{2,1,0:T(8,128)(2,1)S(1)}, bf16[8,128,512]{2,1,0:T(8,128)(2,1)}, u32[]{:S(2)}) copy-start(bf16[8,128,512]{2,1,0:T(8,128)(2,1)} %keys.1) | copy-start | bytes 3145732
  16.3 34.0 %copy-start.1 = (bf16[8,128,512]{2,1,0:T(8,128)(2,1)S(1)}, bf16[8,128,512]{2,1,0:T(8,128)(2,1)}, u32[]{:S(2)}) copy-start(bf16[8,128,512]{2,1,0:T(8,128)(2,1)} %values.1) | copy-start | bytes 3145732
  17.2 17.3 %all-to-all-start.1 = ((bf16[16,16,128]{2,1,0:T(8,128)(2,1)}), bf16[16,16,128]{2,1,0:T(8,128)(2,1)S(1)}, u32[]{:S(2)}, u32[]{:S(2)}) async-start(bf16[16,16,128]{2,1,0:T(8,128)(2,1)} %shard_map.174), calls=%async_computation.1 | async-start | bytes 131072 | tf_op jit(solution)/shard_map/all_to_all | solution.py:301
  25.9 1.0 %copy-start.3 = (bf16[5120,32]{0,1:T(8,128)(2,1)S(1)}, bf16[5120,32]{0,1:T(8,128)(2,1)}, u32[]{:S(2)}) copy-start(bf16[5120,32]{0,1:T(8,128)(2,1)} %param.23) | copy-start | bytes 983044
  26.8 1.0 %copy-start.4 = (bf16[5120,32]{0,1:T(8,128)(2,1)S(1)}, bf16[5120,32]{0,1:T(8,128)(2,1)}, u32[]{:S(2)}) copy-start(bf16[5120,32]{0,1:T(8,128)(2,1)} %param.24) | copy-start | bytes 983044
  30.4 37.1 %copy-start.9 = (bf16[128]{0:T(256)(128)(2,1)S(1)}, bf16[128]{0:T(256)(128)(2,1)}, u32[]{:S(2)}) copy-start(bf16[128]{0:T(256)(128)(2,1)} %gain.3) | copy-start | bytes 772
  35.7 14.6 %all-to-all-start.2 = ((bf16[16,64,128]{2,1,0:T(8,128)(2,1)}), bf16[16,64,128]{2,1,0:T(8,128)(2,1)S(1)}, u32[]{:S(2)}, u32[]{:S(2)}) async-start(bf16[16,64,128]{2,1,0:T(8,128)(2,1)} %get-tuple-element.22), calls=%async_computation.2 | async-start | bytes 524288 | tf_op jit(solution)/shard_map/all_to_all | solution.py:301
  53.8 15.0 %all-to-all-start.3 = ((bf16[16,72,128]{2,1,0:T(8,128)(2,1)}), bf16[16,72,128]{2,1,0:T(8,128)(2,1)S(1)}, u32[]{:S(2)}, u32[]{:S(2)}) async-start(bf16[16,72,128]{2,1,0:T(8,128)(2,1)} %shard_map.177), calls=%async_computation.3 | async-start | bytes 589824 | tf_op jit(solution)/shard_map/all_to_all | solution.py:301
  58.3 9.2 %collective-permute-start.2 = (bf16[16,128]{1,0:T(8,128)(2,1)S(1)}, bf16[16,128]{1,0:T(8,128)(2,1)S(1)}, u32[]{:S(2)}, u32[]{:S(2)}) collective-permute-start(bf16[16,128]{1,0:T(8,128)(2,1)S(1)} %get-tuple-element.23.near), channel_id=1, source_target_pairs={{0,3},{1,2},{2,1},{3,0},{4,7},{5,6},{6,5},{7,4},{8,11},{9,10},{10,... | collective-permute-start | bytes 12296 | tf_op jit(solution)/shard_map/ppermute | solution.py:390
  62.0 5.4 %collective-permute-start.1 = (bf16[16,128]{1,0:T(8,128)(2,1)S(1)}, bf16[16,128]{1,0:T(8,128)(2,1)S(1)}, u32[]{:S(2)}, u32[]{:S(2)}) collective-permute-start(bf16[16,128]{1,0:T(8,128)(2,1)S(1)} %get-tuple-element.23.near), channel_id=1, source_target_pairs={{0,2},{1,3},{2,0},{3,1},{4,6},{5,7},{6,4},{7,5},{8,10},{9,11},{10,... | collective-permute-start | bytes 12296 | tf_op jit(solution)/shard_map/ppermute | solution.py:390
  62.0 5.4 %collective-permute-start = (bf16[16,128]{1,0:T(8,128)(2,1)S(1)}, bf16[16,128]{1,0:T(8,128)(2,1)S(1)}, u32[]{:S(2)}, u32[]{:S(2)}) collective-permute-start(bf16[16,128]{1,0:T(8,128)(2,1)S(1)} %get-tuple-element.23.near), channel_id=1, source_target_pairs={{0,1},{1,0},{2,3},{3,2},{4,5},{5,4},{6,7},{7,6},{8,9},{9,8},{10,11... | collective-permute-start | bytes 12296 | tf_op jit(solution)/shard_map/ppermute | solution.py:390

commit v3 on v2

--- a/solution.py
+++ b/solution.py
@@ -80,14 +80,26 @@
         packed[i] = block
 
 
-def normed_body(
-    lengths, x_any, gain_any, inverse_any, normed, cosines, sines, x_ref, gain, inverse, sems
+CHUNKS = 4
+
+
+def prepare_body(
+    lengths, x_any, gain_any, inverse_any, query_any, key_any, value_any,
+    normed, cosines, sines, base, x_ref, gain, inverse, query_w, key_w, value_w, sems,
 ):
-    for copy in fetch((x_any, gain_any, inverse_any), (x_ref, gain, inverse), sems):
+    step = query_any.shape[0] // CHUNKS
+    rows = [pl.ds(c * step, step) for c in range(CHUNKS)]
+    copies = fetch(
+        [x_any, gain_any, inverse_any, key_any, value_any] + [query_any.at[r] for r in rows],
+        [x_ref, gain, inverse, key_w, value_w] + [query_w.at[r] for r in rows],
+        sems,
+    )
+    for copy in copies[:3]:
         copy.wait()
     x = x_ref[...].astype(F32).reshape(ROWS * TOKENS, -1)
     scale = lax.rsqrt(jnp.mean(x * x, axis=-1, keepdims=True) + EPS)
-    normed[...] = (x * scale * gain[...].astype(F32).reshape(1, -1)).astype(BF16)
+    value = (x * scale * gain[...].astype(F32).reshape(1, -1)).astype(BF16)
+    normed[...] = value
     row, lane = iotas((ROWS * TOKENS, HEAD))
     position = row % TOKENS
     for b in range(ROWS):
@@ -95,6 +107,16 @@
     angles = position.astype(F32) * inverse[...]
     cosines[...] = jnp.cos(angles)
     sines[...] = jnp.where(lane < 64, -1.0, 1.0) * jnp.sin(angles)
+    copies[3].wait()
+    copies[4].wait()
+    both = jnp.concatenate([key_w[...], value_w[...]], axis=0)
+    base[:, 256:384] = widen(dot(value, both, (1, 1)), 128)
+    raw = jnp.zeros((32, 256), F32)
+    for c in range(CHUNKS):
+        copies[5 + c].wait()
+        part = slice(c * step, (c + 1) * step)
+        raw = raw + dot(value[:, part], query_w[part, :])
+    base[:, 0:256] = raw
 
 
 def low_body(packed, normed, low):
@@ -105,35 +127,11 @@
         low[t] = block
 
 
-CHUNKS = 4
-
-
-def base_body(
-    packed, normed, query_any, key_any, value_any, base, ups, out_down, out_up,
-    query_w, key_w, value_w, sems,
-):
-    step = query_any.shape[0] // CHUNKS
-    rows = [pl.ds(c * step, step) for c in range(CHUNKS)]
-    copies = fetch(
-        [query_any.at[r] for r in rows] + [key_any, value_any],
-        [query_w.at[r] for r in rows] + [key_w, value_w],
-        sems,
-    )
+def unpack_body(packed, ups, out_down, out_up):
     pieces = [packed[g].astype(F32) for g in range(GROUPS)]
     out_down[...] = jnp.concatenate([p[12:16, 0:256] for p in pieces], axis=0).astype(BF16)
     ups[...] = jnp.concatenate([p[16:20] for p in pieces], axis=0).astype(BF16)
     out_up[...] = jnp.concatenate([p[20:24] for p in pieces], axis=0).astype(BF16)
-    value = normed[...]
-    raw = jnp.zeros((32, 256), F32)
-    for c in range(CHUNKS):
-        copies[c].wait()
-        part = slice(c * step, (c + 1) * step)
-        raw = raw + dot(value[:, part], query_w[part, :])
-    base[:, 0:256] = raw
-    copies[CHUNKS].wait()
-    copies[CHUNKS + 1].wait()
-    both = jnp.concatenate([key_w[...], value_w[...]], axis=0)
-    base[:, 256:384] = widen(dot(value, both, (1, 1)), 128)
 
 
 def rms_rope(heads, gain, cosines, sines):
@@ -178,8 +176,9 @@
 
 def softmax_parts(scores, usable):
     masked = jnp.where(usable, scores, -1e30)
-    highest = jnp.max(masked, axis=-1, keepdims=True).astype(BF16).astype(F32)
-    weights = jnp.where(usable, jnp.exp(masked - highest), 0.0).astype(BF16)
+    highest = jnp.maximum(jnp.max(masked, axis=-1, keepdims=True), -1e29)
+    highest = highest.astype(BF16).astype(F32)
+    weights = jnp.exp(masked - highest).astype(BF16)
     total = jnp.sum(weights.astype(F32), axis=-1, keepdims=True)
     return highest, weights, total
 
@@ -193,28 +192,30 @@
     everything = [gathered[t].astype(F32) for t in range(PARTS)]
     _, lane = iotas((128, 128))
     stats = jnp.zeros((128, 128), F32)
+    empty = jnp.zeros((32, 128), BF16)
     found = []
     for b in range(ROWS):
         query = jnp.concatenate(
             [q[b * 8 : (b + 1) * 8] for q in everything], axis=0
         ).astype(BF16)
-        scores = jnp.concatenate(
+        query = jnp.concatenate(
             [
-                dot(query[n * 32 : (n + 1) * 32], keys[b, :, n * HEAD : (n + 1) * HEAD], (1, 1))
+                jnp.concatenate(
+                    [query[n * 32 : (n + 1) * 32] if m == n else empty for m in range(4)], axis=1
+                )
                 for n in range(4)
             ],
             axis=0,
         )
+        scores = dot(query, keys[b], (1, 1))
         highest, weights, total = softmax_parts(scores * SCALING, lane + offset < lengths[b])
         total_high = total.astype(BF16).astype(F32)
         stats = jnp.where(lane == b, highest, stats)
         stats = jnp.where(lane == 8 + b, total_high, stats)
         stats = jnp.where(lane == 16 + b, total - total_high, stats)
+        weighted = dot(weights, values[b])
         found.append(
-            [
-                dot(weights[n * 32 : (n + 1) * 32], values[b, :, n * HEAD : (n + 1) * HEAD])
-                for n in range(4)
-            ]
+            [weighted[n * 32 : (n + 1) * 32, n * HEAD : (n + 1) * HEAD] for n in range(4)]
         )
     for t in range(PARTS):
         rows = slice(t % 4 * 8, t % 4 * 8 + 8)
@@ -251,14 +252,15 @@
     stats_out[...] = stats
 
 
+def load_body(source, held, sem):
+    copy = pltpu.make_async_copy(source, held, sem)
+    copy.start()
+    copy.wait()
+
+
 def output_body(
-    gathered, own_weighted, own_stats, output_any, out_down, packed, output_w, sems
+    gathered, own_weighted, own_stats, output_w, out_down, packed
 ):
-    step = output_any.shape[1] // CHUNKS
-    parts = [pl.ds(c * step, step) for c in range(CHUNKS)]
-    copies = fetch(
-        [output_any.at[:, part] for part in parts], [output_w.at[:, part] for part in parts], sems
-    )
     blocks = [gathered[t].astype(F32) for t in range(PARTS)]
     stats = [block[64:72] for block in blocks] + [own_stats[...]]
     values = [block[0:64] for block in blocks] + [own_weighted[...]]
@@ -279,13 +281,10 @@
     heads = dot(regroup(2, 8), heads).astype(BF16)
     heads = jnp.concatenate([heads[0:32], heads[32:64]], axis=1)
     low = dot(heads, out_down[...], (1, 1))
-    share = PARTS // CHUNKS
-    for c in range(CHUNKS):
-        copies[c].wait()
-        partial = dot(heads, output_w[:, c * step : (c + 1) * step])
-        for t in range(share):
-            block = jnp.concatenate([partial[:, t * 320 : (t + 1) * 320], low], axis=1)
-            packed[c * share + t] = block.astype(BF16)
+    partial = dot(heads, output_w[...])
+    for t in range(PARTS):
+        block = jnp.concatenate([partial[:, t * 320 : (t + 1) * 320], low], axis=1)
+        packed[t] = block.astype(BF16)
 
 
 def finish_body(gathered, out_up, result):
@@ -343,39 +342,44 @@
 
     inverse = THETA ** (-(np.arange(64, dtype=np.float64) * 2.0 / HEAD))
     inverse = jnp.asarray(np.concatenate([inverse, inverse]).reshape(1, HEAD), F32)
-    normed, cosines, sines = call(
-        normed_body,
-        (SHAPE((32, width), BF16), SHAPE((32, HEAD), F32), SHAPE((32, HEAD), F32)),
-        (filled_lengths, layer_inputs, input_norm_gain, inverse),
-        "saaa",
-        12,
+    normed, cosines, sines, base = call(
+        prepare_body,
+        (
+            SHAPE((32, width), BF16),
+            SHAPE((32, HEAD), F32),
+            SHAPE((32, HEAD), F32),
+            SHAPE((32, 384), F32),
+        ),
+        (
+            filled_lengths,
+            layer_inputs,
+            input_norm_gain,
+            inverse,
+            query_matrix,
+            key_matrix.T,
+            value_matrix.T,
+        ),
+        "saaaaaa",
+        10.75,
         [
             pltpu.VMEM(layer_inputs.shape, BF16),
             pltpu.VMEM((width,), BF16),
             pltpu.VMEM((1, HEAD), F32),
-            dma((3,)),
-        ],
-        moved=WINDOW,
-    )
-    low = call(low_body, SHAPE((PARTS, 16, 128), BF16), (packed, normed), "vv", 20)
-    low = swap(low, TP)
-    base, ups, out_down, out_up = call(
-        base_body,
-        (
-            SHAPE((32, 384), F32),
-            SHAPE((64, 384), BF16),
-            SHAPE((64, 256), BF16),
-            SHAPE((64, 384), BF16),
-        ),
-        (packed, normed, query_matrix, key_matrix.T, value_matrix.T),
-        "vvaaa",
-        12,
-        [
             pltpu.VMEM(query_matrix.shape, BF16),
             pltpu.VMEM((32, width), BF16),
             pltpu.VMEM((32, width), BF16),
-            dma((CHUNKS + 2,)),
+            dma((5 + CHUNKS,)),
         ],
+        moved=WINDOW,
+    )
+    low = call(low_body, SHAPE((PARTS, 16, 128), BF16), (packed, normed), "vv", 20)
+    low = swap(low, TP)
+    ups, out_down, out_up = call(
+        unpack_body,
+        (SHAPE((64, 384), BF16), SHAPE((64, 256), BF16), SHAPE((64, 384), BF16)),
+        (packed,),
+        "v",
+        20,
         moved=WINDOW,
     )
     queries, own, fresh = call(
@@ -389,14 +393,6 @@
     fresh = [fresh] + [
         lax.ppermute(fresh, "near", [(i, i ^ k) for i in range(4)]) for k in range(1, 4)
     ]
-    parts = call(
-        attend_body,
-        SHAPE((PARTS, 72, 128), BF16),
-        (place, filled_lengths, gathered, stored_keys, stored_values),
-        "ssvvv",
-        20,
-    )
-    parts = swap(parts, TP)
     own_weighted, own_stats = call(
         fresh_body,
         (SHAPE((64, 128), F32), SHAPE((8, 128), F32)),
@@ -406,13 +402,27 @@
         [pltpu.VMEM((4, 16, 128), F32)],
         moved=WINDOW,
     )
+    gathered, own_weighted, own_stats = lax.optimization_barrier(
+        (gathered, own_weighted, own_stats)
+    )
+    parts = call(
+        attend_body,
+        SHAPE((PARTS, 72, 128), BF16),
+        (place, filled_lengths, gathered, stored_keys, stored_values),
+        "ssvvv",
+        20,
+    )
+    parts, output_late = lax.optimization_barrier((parts, output_matrix))
+    parts = swap(parts, TP)
+    output_late = call(
+        load_body, SHAPE(output_matrix.shape, BF16), (output_late,), "a", 14, [dma], moved=WINDOW
+    )
     partial = call(
         output_body,
         SHAPE((PARTS, 32, 384), BF16),
-        (parts, own_weighted, own_stats, output_matrix, out_down),
-        "vvvav",
-        12,
-        [pltpu.VMEM(output_matrix.shape, BF16), dma((CHUNKS,))],
+        (parts, own_weighted, own_stats, output_late, out_down),
+        "vvvvv",
+        20,
     )
     partial = swap(partial, TP)
     return call(finish_body, SHAPE((ROWS, TOKENS, 320), BF16), (partial, out_up), "vv", 20)

time: 90.7 us -> 86.4 us (0.953)
  local copies, waits for them, and re-layouts: 4.94 us -> 2.03 us
  blocking collectives: 17.6 us -> 16.5 us
  Pallas kernels: 15 us -> 13.9 us
    unnamed x22 -> x16, local copies, waits for them, and re-layouts: 4.94 us -> 2.03 us
    all_to_all x4, waiting for transfers between devices: 18.6 us -> 20 us  [swap(): return lax.all_to_all(block, axis, 0, 0)]
    pallas_call x9 -> x10, Pallas kernels: 15 us -> 13.9 us  [call(): pl.pallas_call(body, out_shape=out_shapes, in_specs=specs, out_specs=tupl...]
    all_to_all x1, blocking collectives: 17.6 us -> 16.5 us  [swap(): return lax.all_to_all(block, axis, 0, 0)]
  transfers between devices with their start and end apart: 7 -> 7, of which waited for: 5 -> 5; matrix products, arithmetic and copies ran while one was open for 0% -> 0% of each run, Pallas kernels for 5% -> 7%
where the time goes in v3:
time: 86.4 us; the launch traced here: 85.8 us
  starting transfers between devices  29.6 us (34%)
  waiting for transfers between devices  23.8 us (28%)
  blocking collectives  16.5 us (19%)
  Pallas kernels  13.9 us (16%)
  local copies, waits for them, and re-layouts  2.03 us (2%)
    all_to_all x4, starting transfers between devices, swap(): return lax.all_to_all(block, axis, 0, 0)  25.1 us
    all_to_all x4, waiting for transfers between devices, swap(): return lax.all_to_all(block, axis, 0, 0)  20 us
    all_to_all x1, blocking collectives, swap(): return lax.all_to_all(block, axis, 0, 0)  16.5 us
    pallas_call x10, Pallas kernels, call(): pl.pallas_call(body, out_shape=out_shapes, in_specs=specs, out_specs=tupl...  13.9 us
    ppermute x3, starting transfers between devices, local(): lax.ppermute(fresh, 'near', [(i, i ^ k) for i in range(4)])  4.47 us
    ppermute x3, waiting for transfers between devices, local(): lax.ppermute(fresh, 'near', [(i, i ^ k) for i in range(4)])  3.8 us
    unnamed x16, local copies, waits for them, and re-layouts  2.03 us
  transfers between devices with their start and end apart: 7, of which 5 were waited for; matrix products, arithmetic and copies ran while one was open for 0% of the time, Pallas kernels for 7%

profile of v3, /device:TPU:2, one launch (start us, length us, event | category | flops | bytes accessed | tf_op | source)
XLA Modules:
  0.0 85.8 jit_solution(12959470905194614260)
XLA Ops:
  0.0 1.6 %shard_map.172 = bf16[16,24,384]{2,1,0:T(8,128)(2,1)} custom-call(bf16[12,320]{1,0:T(8,128)(2,1)} %bitcast.7, bf16[4,256]{1,0:T(4,128)(2,1)} %bitcast.8, bf16[4,256]{1,0:T(4,128)(2,1)} %refs_2_.1, bf16[4,32]{1,0:T(4,128)(2,1)} %refs_3_.1, bf16[4,32]{1,0:T(4,128)(2,1)} %refs_4_.1, bf16[4,320]{1,0:T(4,128)(2,1)} %refs_5_.1), custom_call_target="tpu_custom_call" | custom-call | tf_op jit(solution)/shard_map/pallas_call | solution.py:36
  1.6 0.0 copy-start.5
  1.6 7.5 %all-to-all-start = ((bf16[16,24,384]{2,1,0:T(8,128)(2,1)}), bf16[16,24,384]{2,1,0:T(8,128)(2,1)S(1)}, u32[]{:S(2)}, u32[]{:S(2)}) async-start(bf16[16,24,384]{2,1,0:T(8,128)(2,1)} %shard_map.172), calls=%async_computation | async-start | bytes 589824 | tf_op jit(solution)/shard_map/all_to_all | solution.py:300
  9.1 0.7 copy-done.2
  9.8 0.7 copy-done.3
  10.5 0.7 copy-done.7
  11.1 3.4 %shard_map.173 = (bf16[32,5120]{1,0:T(8,128)(2,1)S(1)}, f32[32,128]{1,0:T(8,128)S(1)}, f32[32,128]{1,0:T(8,128)S(1)}, f32[32,384]{1,0:T(8,128)S(1)}) custom-call(s32[8]{0:T(128)S(1)} %copy-done.3, bf16[8,4,5120]{2,1,0:T(4,128)(2,1)} %x_any.1, bf16[5120]{0:T(1024)(128)(2,1)S(1)} %copy-done.2, f32[1,128]{1,0:T(1,128)S(1)} %copy-done.7, ...), custom_call_target="tpu_custom_call" | custom-call | bytes 16777216 | tf_op jit(solution)/shard_map/pallas_call | solution.py:36
  14.5 1.8 %all-to-all-done.packed = bf16[16,24,384]{2,1,0:T(8,128)(2,1)S(1)} async-done(((bf16[16,24,384]{2,1,0:T(8,128)(2,1)}), bf16[16,24,384]{2,1,0:T(8,128)(2,1)S(1)}, u32[]{:S(2)}, u32[]{:S(2)}) %all-to-all-start) | async-done | bytes 294944 | tf_op jit(solution)/shard_map/all_to_all | solution.py:300
  16.3 0.9 %shard_map.174 = bf16[16,16,128]{2,1,0:T(8,128)(2,1)} custom-call(bf16[16,24,384]{2,1,0:T(8,128)(2,1)S(1)} %all-to-all-done.packed, bf16[32,5120]{1,0:T(8,128)(2,1)S(1)} %get-tuple-element.22.normed), custom_call_target="tpu_custom_call" | custom-call | tf_op jit(solution)/shard_map/pallas_call | solution.py:36
  17.2 8.7 %all-to-all-start.1 = ((bf16[16,16,128]{2,1,0:T(8,128)(2,1)}), bf16[16,16,128]{2,1,0:T(8,128)(2,1)S(1)}, u32[]{:S(2)}, u32[]{:S(2)}) async-start(bf16[16,16,128]{2,1,0:T(8,128)(2,1)} %shard_map.174), calls=%async_computation.1 | async-start | bytes 131072 | tf_op jit(solution)/shard_map/all_to_all | solution.py:300
  25.9 8.6 %all-to-all-done.1.low = bf16[16,16,128]{2,1,0:T(8,128)(2,1)S(1)} async-done(((bf16[16,16,128]{2,1,0:T(8,128)(2,1)}), bf16[16,16,128]{2,1,0:T(8,128)(2,1)S(1)}, u32[]{:S(2)}, u32[]{:S(2)}) %all-to-all-start.1) | async-done | bytes 65568 | tf_op jit(solution)/shard_map/all_to_all | solution.py:300
  34.5 0.0 copy-done.5
  34.5 1.2 %shard_map.176 = (bf16[16,64,128]{2,1,0:T(8,128)(2,1)}, bf16[64,128]{1,0:T(8,128)(2,1)S(1)}, bf16[16,128]{1,0:T(8,128)(2,1)S(1)}) custom-call(bf16[16,16,128]{2,1,0:T(8,128)(2,1)S(1)} %all-to-all-done.1.low, f32[32,384]{1,0:T(8,128)S(1)} %get-tuple-element.23.base, bf16[64,384]{1,0:T(8,128)(2,1)S(1)} %get-tuple-element.24.ups, ...), custom_call_target="tpu_custom_call" | custom-call | tf_op jit(solution)/shard_map/pallas_call | solution.py:36
  35.7 3.5 %all-to-all-start.2 = ((bf16[16,64,128]{2,1,0:T(8,128)(2,1)}), bf16[16,64,128]{2,1,0:T(8,128)(2,1)S(1)}, u32[]{:S(2)}, u32[]{:S(2)}) async-start(bf16[16,64,128]{2,1,0:T(8,128)(2,1)} %get-tuple-element.27), calls=%async_computation.2 | async-start | bytes 524288 | tf_op jit(solution)/shard_map/all_to_all | solution.py:300
  39.2 3.6 %collective-permute-start.2 = (bf16[16,128]{1,0:T(8,128)(2,1)S(1)}, bf16[16,128]{1,0:T(8,128)(2,1)S(1)}, u32[]{:S(2)}, u32[]{:S(2)}) collective-permute-start(bf16[16,128]{1,0:T(8,128)(2,1)S(1)} %get-tuple-element.28.near), channel_id=1, source_target_pairs={{0,3},{1,2},{2,1},{3,0},{4,7},{5,6},{6,5},{7,4},{8,11},{9,10},{10,... | collective-permute-start | bytes 12296 | tf_op jit(solution)/shard_map/ppermute | solution.py:394
  42.8 0.0 collective-permute-start.1
  42.8 0.9 collective-permute-start
  43.7 3.8 %collective-permute-done.2.near_3 = bf16[16,128]{1,0:T(8,128)(2,1)S(1)} collective-permute-done((bf16[16,128]{1,0:T(8,128)(2,1)S(1)}, bf16[16,128]{1,0:T(8,128)(2,1)S(1)}, u32[]{:S(2)}, u32[]{:S(2)}) %collective-permute-start.2) | collective-permute-done | bytes 4128 | tf_op jit(solution)/shard_map/ppermute | solution.py:394
  47.5 0.0 collective-permute-done.1.near_2
  47.5 0.0 collective-permute-done.near_1
  47.5 0.0 copy-done.6
  47.5 0.6 shard_map.177
  48.1 1.0 %all-to-all-done.2.gathered = bf16[16,64,128]{2,1,0:T(8,128)(2,1)S(1)} async-done(((bf16[16,64,128]{2,1,0:T(8,128)(2,1)}), bf16[16,64,128]{2,1,0:T(8,128)(2,1)S(1)}, u32[]{:S(2)}, u32[]{:S(2)}) %all-to-all-start.2) | async-done | bytes 262176 | tf_op jit(solution)/shard_map/all_to_all | solution.py:300
  49.1 0.0 copy-done
  49.1 0.0 copy-done.4
  49.1 2.4 %shard_map.178 = bf16[16,72,128]{2,1,0:T(8,128)(2,1)} custom-call(s32[1]{0:T(128)} %bitcast.place, s32[8]{0:T(128)S(1)} %copy-done.4, bf16[16,64,128]{2,1,0:T(8,128)(2,1)S(1)} %all-to-all-done.2.gathered, bf16[8,128,512]{2,1,0:T(8,128)(2,1)S(1)} %copy-done, bf16[8,128,512]{2,1,0:T(8,128)(2,1)S(1)} %copy-done.1), custom_call_target="tpu_custom_call" | custom-call | tf_op jit(solution)/shard_map/pallas_call | solution.py:36
  51.6 5.4 %all-to-all-start.3 = ((bf16[16,72,128]{2,1,0:T(8,128)(2,1)}), bf16[16,72,128]{2,1,0:T(8,128)(2,1)S(1)}, u32[]{:S(2)}, u32[]{:S(2)}) async-start(bf16[16,72,128]{2,1,0:T(8,128)(2,1)} %shard_map.178), calls=%async_computation.3 | async-start | bytes 589824 | tf_op jit(solution)/shard_map/all_to_all | solution.py:300
  57.0 1.8 %shard_map.179.output_w = bf16[256,5120]{1,0:T(8,128)(2,1)S(1)} custom-call(bf16[256,5120]{1,0:T(8,128)(2,1)} %source), custom_call_target="tpu_custom_call" | custom-call | bytes 16777216 | tf_op jit(solution)/shard_map/pallas_call | solution.py:36
  58.7 8.6 %all-to-all-done.3.gathered = bf16[16,72,128]{2,1,0:T(8,128)(2,1)S(1)} async-done(((bf16[16,72,128]{2,1,0:T(8,128)(2,1)}), bf16[16,72,128]{2,1,0:T(8,128)(2,1)S(1)}, u32[]{:S(2)}, u32[]{:S(2)}) %all-to-all-start.3) | async-done | bytes 294944 | tf_op jit(solution)/shard_map/all_to_all | solution.py:300
  67.4 1.1 %shard_map.180 = bf16[16,32,384]{2,1,0:T(8,128)(2,1)S(1)} custom-call(bf16[16,72,128]{2,1,0:T(8,128)(2,1)S(1)} %all-to-all-done.3.gathered, f32[64,128]{1,0:T(8,128)S(1)} %get-tuple-element.34.own_weighted, f32[8,128]{1,0:T(8,128)S(1)} %get-tuple-element.35.own_stats, bf16[256,5120]{1,0:T(8,128)(2,1)S(1)} %shard_map.179.output_w, ...), custom_call_target="tpu_custom_call" | custom-call | tf_op jit(solution)/shard_map/pallas_call | solution.py:36
  68.5 16.5 %all_to_all.25.gathered = bf16[16,32,384]{2,1,0:T(8,128)(2,1)S(1)} all-to-all(bf16[16,32,384]{2,1,0:T(8,128)(2,1)S(1)} %shard_map.180), channel_id=1, replica_groups=mesh['group'=16,'far'=4,'near'=4] {'far','near'}, dimensions={0} | all-to-all | bytes 786432 | tf_op jit(solution)/shard_map/all_to_all | solution.py:300
  85.0 0.8 shard_map.181
  (9 shorter events, 0.1 us)
Async XLA Ops:
  1.6 32.9 %copy-start.5 = (bf16[128]{0:T(256)(128)(2,1)S(1)}, bf16[128]{0:T(256)(128)(2,1)}, u32[]{:S(2)}) copy-start(bf16[128]{0:T(256)(128)(2,1)} %gain.2) | copy-start | bytes 772
  1.6 14.7 %all-to-all-start = ((bf16[16,24,384]{2,1,0:T(8,128)(2,1)}), bf16[16,24,384]{2,1,0:T(8,128)(2,1)S(1)}, u32[]{:S(2)}, u32[]{:S(2)}) async-start(bf16[16,24,384]{2,1,0:T(8,128)(2,1)} %shard_map.172), calls=%async_computation | async-start | bytes 589824 | tf_op jit(solution)/shard_map/all_to_all | solution.py:300
  9.1 0.7 copy-start.2
  9.8 0.7 copy-start.3
  10.5 0.7 copy-start.7
  11.1 36.4 %copy-start.6 = (bf16[128]{0:T(256)(128)(2,1)S(1)}, bf16[128]{0:T(256)(128)(2,1)}, u32[]{:S(2)}) copy-start(bf16[128]{0:T(256)(128)(2,1)} %gain.3) | copy-start | bytes 772
  11.1 38.0 %copy-start = (bf16[8,128,512]{2,1,0:T(8,128)(2,1)S(1)}, bf16[8,128,512]{2,1,0:T(8,128)(2,1)}, u32[]{:S(2)}) copy-start(bf16[8,128,512]{2,1,0:T(8,128)(2,1)} %keys.1) | copy-start | bytes 3145732
  11.1 38.0 %copy-start.1 = (bf16[8,128,512]{2,1,0:T(8,128)(2,1)S(1)}, bf16[8,128,512]{2,1,0:T(8,128)(2,1)}, u32[]{:S(2)}) copy-start(bf16[8,128,512]{2,1,0:T(8,128)(2,1)} %values.1) | copy-start | bytes 3145732
  11.1 38.0 %copy-start.4 = (s32[8]{0:T(128)S(1)}, s32[8]{0:T(128)}, u32[]{:S(2)}) copy-start(s32[8]{0:T(128)} %lengths.3) | copy-start | bytes 100
  17.2 17.3 %all-to-all-start.1 = ((bf16[16,16,128]{2,1,0:T(8,128)(2,1)}), bf16[16,16,128]{2,1,0:T(8,128)(2,1)S(1)}, u32[]{:S(2)}, u32[]{:S(2)}) async-start(bf16[16,16,128]{2,1,0:T(8,128)(2,1)} %shard_map.174), calls=%async_computation.1 | async-start | bytes 131072 | tf_op jit(solution)/shard_map/all_to_all | solution.py:300
  35.7 13.4 %all-to-all-start.2 = ((bf16[16,64,128]{2,1,0:T(8,128)(2,1)}), bf16[16,64,128]{2,1,0:T(8,128)(2,1)S(1)}, u32[]{:S(2)}, u32[]{:S(2)}) async-start(bf16[16,64,128]{2,1,0:T(8,128)(2,1)} %get-tuple-element.27), calls=%async_computation.2 | async-start | bytes 524288 | tf_op jit(solution)/shard_map/all_to_all | solution.py:300
  39.2 8.3 %collective-permute-start.2 = (bf16[16,128]{1,0:T(8,128)(2,1)S(1)}, bf16[16,128]{1,0:T(8,128)(2,1)S(1)}, u32[]{:S(2)}, u32[]{:S(2)}) collective-permute-start(bf16[16,128]{1,0:T(8,128)(2,1)S(1)} %get-tuple-element.28.near), channel_id=1, source_target_pairs={{0,3},{1,2},{2,1},{3,0},{4,7},{5,6},{6,5},{7,4},{8,11},{9,10},{10,... | collective-permute-start | bytes 12296 | tf_op jit(solution)/shard_map/ppermute | solution.py:394
  42.8 4.7 %collective-permute-start.1 = (bf16[16,128]{1,0:T(8,128)(2,1)S(1)}, bf16[16,128]{1,0:T(8,128)(2,1)S(1)}, u32[]{:S(2)}, u32[]{:S(2)}) collective-permute-start(bf16[16,128]{1,0:T(8,128)(2,1)S(1)} %get-tuple-element.28.near), channel_id=1, source_target_pairs={{0,2},{1,3},{2,0},{3,1},{4,6},{5,7},{6,4},{7,5},{8,10},{9,11},{10,... | collective-permute-start | bytes 12296 | tf_op jit(solution)/shard_map/ppermute | solution.py:394
  42.8 4.7 %collective-permute-start = (bf16[16,128]{1,0:T(8,128)(2,1)S(1)}, bf16[16,128]{1,0:T(8,128)(2,1)S(1)}, u32[]{:S(2)}, u32[]{:S(2)}) collective-permute-start(bf16[16,128]{1,0:T(8,128)(2,1)S(1)} %get-tuple-element.28.near), channel_id=1, source_target_pairs={{0,1},{1,0},{2,3},{3,2},{4,5},{5,4},{6,7},{7,6},{8,9},{9,8},{10,11... | collective-permute-start | bytes 12296 | tf_op jit(solution)/shard_map/ppermute | solution.py:394
  51.6 15.8 %all-to-all-start.3 = ((bf16[16,72,128]{2,1,0:T(8,128)(2,1)}), bf16[16,72,128]{2,1,0:T(8,128)(2,1)S(1)}, u32[]{:S(2)}, u32[]{:S(2)}) async-start(bf16[16,72,128]{2,1,0:T(8,128)(2,1)} %shard_map.178), calls=%async_computation.3 | async-start | bytes 589824 | tf_op jit(solution)/shard_map/all_to_all | solution.py:300

commit v4 on v3

--- a/solution.py
+++ b/solution.py
@@ -7,7 +7,6 @@
 from jax import lax
 from jax.experimental import pallas as pl
 from jax.experimental.pallas import tpu as pltpu
-from jax.sharding import Mesh
 from jax.sharding import PartitionSpec as P
 
 EPS = 1e-06
@@ -15,7 +14,6 @@
 THETA = 1000000.0
 GROUPS = 16
 PARTS = 16
-TP = ("far", "near")
 HEAD = 128
 TOKENS = 4
 ROWS = 8
@@ -85,7 +83,7 @@
 
 def prepare_body(
     lengths, x_any, gain_any, inverse_any, query_any, key_any, value_any,
-    normed, cosines, sines, base, x_ref, gain, inverse, query_w, key_w, value_w, sems,
+    normed, cosines, sines, base, fresh, x_ref, gain, inverse, query_w, key_w, value_w, sems,
 ):
     step = query_any.shape[0] // CHUNKS
     rows = [pl.ds(c * step, step) for c in range(CHUNKS)]
@@ -110,27 +108,45 @@
     copies[3].wait()
     copies[4].wait()
     both = jnp.concatenate([key_w[...], value_w[...]], axis=0)
-    base[:, 256:384] = widen(dot(value, both, (1, 1)), 128)
+    fresh[...] = widen(dot(value, both, (1, 1)), 128)
     raw = jnp.zeros((32, 256), F32)
     for c in range(CHUNKS):
         copies[5 + c].wait()
         part = slice(c * step, (c + 1) * step)
         raw = raw + dot(value[:, part], query_w[part, :])
-    base[:, 0:256] = raw
-
-
-def low_body(packed, normed, low):
-    pieces = [packed[g, 0:16, 0:320].astype(F32) for g in range(GROUPS)]
-    down = jnp.concatenate(pieces, axis=1).astype(BF16)
+    base[...] = raw
+
+
+def fold(block):
+    rows = block.shape[0] // 2
+    _, lane = iotas((rows, 128))
+    return jnp.where(lane < 64, block[0:rows], pltpu.roll(block[rows:], 64, 1))
+
+
+def unfold(block):
+    return jnp.concatenate([block, pltpu.roll(block, 64, 1)], axis=0)
+
+
+def low_body(packed, normed, fresh, low, near):
+    pieces = [packed[g].astype(F32) for g in range(GROUPS)]
+    down = jnp.concatenate([p[0:16, 0:320] for p in pieces], axis=1).astype(BF16)
     block = widen(dot(down, normed[...], (1, 1)), 128).astype(BF16)
     for t in range(PARTS):
         low[t] = block
+    lift = jnp.concatenate([p[16:20, 256:384] for p in pieces], axis=0)
+    near[0:16] = fold(fresh[...]).astype(BF16)
+    near[16:48] = fold(lift).astype(BF16)
 
 
 def unpack_body(packed, ups, out_down, out_up):
     pieces = [packed[g].astype(F32) for g in range(GROUPS)]
     out_down[...] = jnp.concatenate([p[12:16, 0:256] for p in pieces], axis=0).astype(BF16)
-    ups[...] = jnp.concatenate([p[16:20] for p in pieces], axis=0).astype(BF16)
+    lift = jnp.concatenate([p[16:20, 0:256] for p in pieces], axis=0)
+    lift = jnp.concatenate([lift, jnp.zeros((8, 256), F32)], axis=0)
+    rest = jnp.zeros((4, 256), F32)
+    for t in range(6):
+        block = jnp.concatenate([lift[t * 12 : (t + 1) * 12], rest], axis=0)
+        ups[t * 16 : (t + 1) * 16] = block.astype(BF16)
     out_up[...] = jnp.concatenate([p[20:24] for p in pieces], axis=0).astype(BF16)
 
 
@@ -147,17 +163,9 @@
     return jnp.where(col == source, 1.0, 0.0).astype(BF16)
 
 
-def query_body(low, base, ups, cosines, sines, gain, packed, own, fresh):
-    ranks = jnp.concatenate([low[t].astype(F32)[0:12] for t in range(PARTS)], axis=0)
-    ranks = ranks[:, 0:32].astype(BF16)
-    lift = ups[...]
-    _, column = iotas(lift.shape)
-    zero = jnp.zeros_like(lift)
-    lifts = [
-        jnp.where((column >= first) & (column < last), lift, zero)
-        for first, last in ((0, 256), (256, 288), (288, 320))
-    ]
-    update = dot(ranks, jnp.concatenate(lifts, axis=0), (0, 0))
+def query_body(low, base, ups, cosines, sines, gain, packed, own):
+    ranks = low[0:6].reshape(96, 128)[:, 0:32]
+    update = dot(ranks, ups[...], (0, 0))
     raw = base[...] + ADAPTER_SCALE * update
     scale = gain[...].astype(F32).reshape(1, -1)
     heads = [
@@ -169,9 +177,6 @@
     for i in range(PARTS):
         packed[i] = queries
     own[...] = queries
-    _, lane = iotas((16, 128))
-    folded = jnp.where(lane < 64, raw[0:16, 256:384], pltpu.roll(raw[16:32, 256:384], 64, 1))
-    fresh[...] = folded.astype(BF16)
 
 
 def softmax_parts(scores, usable):
@@ -224,18 +229,23 @@
 
 
 def fresh_body(
-    place, near, near_1, near_2, near_3, own, cosines, sines, gain, weighted, stats_out, gathered
+    place, near, near_1, near_2, near_3, low, own, cosines, sines, gain,
+    weighted, stats_out, pieces,
 ):
     for k, piece in enumerate((near, near_1, near_2, near_3)):
-        gathered[(place[0] % 4) ^ k] = piece[...].astype(F32)
+        pieces[(place[0] % 4) ^ k] = piece[...]
+    ranks = [low[t].astype(F32)[0:12] for t in range(PARTS)]
+    ranks = jnp.concatenate(ranks, axis=0)[:, 0:32].astype(BF16)
     fresh_key = []
     fresh_value = []
     for q in range(4):
-        fold = gathered[q]
-        wide = jnp.concatenate([fold, pltpu.roll(fold, 64, 1)], axis=0)
-        fresh_key.append(wide[:, 0:32])
-        fresh_value.append(wide[:, 32:64])
-    new_keys = jnp.concatenate(fresh_key, axis=1)
+        raw = unfold(pieces[q, 0:16].astype(F32))
+        lift = unfold(pieces[q, 16:48].astype(F32)).astype(BF16)
+        key = raw + ADAPTER_SCALE * dot(ranks[64:128], lift, (0, 0))
+        value = raw + ADAPTER_SCALE * dot(ranks[128:192], lift, (0, 0))
+        fresh_key.append(key[:, 0:32])
+        fresh_value.append(value[:, 32:64])
+    new_keys = jnp.concatenate(fresh_key, axis=1).astype(BF16).astype(F32)
     scale = gain[...].astype(F32).reshape(1, -1)
     new_keys = rms_rope(new_keys, scale, cosines[...], sines[...]).astype(BF16)
     new_values = jnp.concatenate(fresh_value, axis=1).astype(BF16)
@@ -321,7 +331,7 @@
 ):
     dma = pltpu.SemaphoreType.DMA
     width = layer_inputs.shape[-1]
-    place = lax.axis_index(TP).astype(jnp.int32).reshape(1)
+    place = lax.axis_index("tp").astype(jnp.int32).reshape(1)
     shards = (
         adapter_down.T,
         output_down_factor.T,
@@ -338,17 +348,19 @@
         8,
         [pltpu.VMEM(s.shape, BF16) for s in shards] + [dma((6,))],
     )
+    packed, place = lax.optimization_barrier((packed, place))
     packed = swap(packed, "group")
 
     inverse = THETA ** (-(np.arange(64, dtype=np.float64) * 2.0 / HEAD))
     inverse = jnp.asarray(np.concatenate([inverse, inverse]).reshape(1, HEAD), F32)
-    normed, cosines, sines, base = call(
+    normed, cosines, sines, base, fresh = call(
         prepare_body,
         (
             SHAPE((32, width), BF16),
             SHAPE((32, HEAD), F32),
             SHAPE((32, HEAD), F32),
-            SHAPE((32, 384), F32),
+            SHAPE((32, 256), F32),
+            SHAPE((32, HEAD), F32),
         ),
         (
             filled_lengths,
@@ -372,39 +384,34 @@
         ],
         moved=WINDOW,
     )
-    low = call(low_body, SHAPE((PARTS, 16, 128), BF16), (packed, normed), "vv", 20)
-    low = swap(low, TP)
+    low, near = call(
+        low_body,
+        (SHAPE((PARTS, 16, 128), BF16), SHAPE((48, 128), BF16)),
+        (packed, normed, fresh),
+        "vvv",
+        20,
+    )
+    low = swap(low, "tp")
+    near = [near] + [
+        lax.ppermute(near, "tp", [(i, i ^ k) for i in range(PARTS)]) for k in range(1, 4)
+    ]
     ups, out_down, out_up = call(
         unpack_body,
-        (SHAPE((64, 384), BF16), SHAPE((64, 256), BF16), SHAPE((64, 384), BF16)),
+        (SHAPE((96, 256), BF16), SHAPE((64, 256), BF16), SHAPE((64, 384), BF16)),
         (packed,),
         "v",
         20,
         moved=WINDOW,
     )
-    queries, own, fresh = call(
+    low, near = lax.optimization_barrier((low, near))
+    queries, own = call(
         query_body,
-        (SHAPE((PARTS, 64, 128), BF16), SHAPE((64, 128), BF16), SHAPE((16, 128), BF16)),
+        (SHAPE((PARTS, 64, 128), BF16), SHAPE((64, 128), BF16)),
         (low, base, ups, cosines, sines, query_norm_gain),
         "vvvvvv",
         20,
     )
-    gathered = swap(queries, TP)
-    fresh = [fresh] + [
-        lax.ppermute(fresh, "near", [(i, i ^ k) for i in range(4)]) for k in range(1, 4)
-    ]
-    own_weighted, own_stats = call(
-        fresh_body,
-        (SHAPE((64, 128), F32), SHAPE((8, 128), F32)),
-        (place, *fresh, own, cosines, sines, key_norm_gain),
-        "svvvvvvvv",
-        20,
-        [pltpu.VMEM((4, 16, 128), F32)],
-        moved=WINDOW,
-    )
-    gathered, own_weighted, own_stats = lax.optimization_barrier(
-        (gathered, own_weighted, own_stats)
-    )
+    gathered = swap(queries, "tp")
     parts = call(
         attend_body,
         SHAPE((PARTS, 72, 128), BF16),
@@ -412,10 +419,19 @@
         "ssvvv",
         20,
     )
-    parts, output_late = lax.optimization_barrier((parts, output_matrix))
-    parts = swap(parts, TP)
+    parts, own, output_late = lax.optimization_barrier((parts, own, output_matrix))
+    parts = swap(parts, "tp")
     output_late = call(
         load_body, SHAPE(output_matrix.shape, BF16), (output_late,), "a", 14, [dma], moved=WINDOW
+    )
+    own_weighted, own_stats = call(
+        fresh_body,
+        (SHAPE((64, 128), F32), SHAPE((8, 128), F32)),
+        (place, *near, low, own, cosines, sines, key_norm_gain),
+        "svvvvvvvvv",
+        20,
+        [pltpu.VMEM((4, 48, 128), BF16)],
+        moved=WINDOW,
     )
     partial = call(
         output_body,
@@ -424,31 +440,29 @@
         "vvvvv",
         20,
     )
-    partial = swap(partial, TP)
+    partial = swap(partial, "tp")
     return call(finish_body, SHAPE((ROWS, TOKENS, 320), BF16), (partial, out_up), "vv", 20)
 
 
 def solution(mesh):
-    fine = Mesh(mesh.devices.reshape(16, 4, 4), ("group", "far", "near"))
-    group, tp = "group", TP
     in_specs = (
-        P(group, None, None),
+        P("group", None, None),
         P(),
         P(),
         P(),
-        P(None, tp),
-        P(None, tp),
-        P(None, tp),
-        P(tp, None),
-        P(group, tp),
-        P(group, tp),
-        P(group, tp),
-        P(group, tp),
-        P(tp, group),
-        P(group, tp),
-        P(group, tp, None),
-        P(group, tp, None),
-        P(group),
-    )
-    out_specs = P(group, None, tp)
-    return jax.shard_map(local, mesh=fine, in_specs=in_specs, out_specs=out_specs, check_vma=False)
+        P(None, "tp"),
+        P(None, "tp"),
+        P(None, "tp"),
+        P("tp", None),
+        P("group", "tp"),
+        P("group", "tp"),
+        P("group", "tp"),
+        P("group", "tp"),
+        P("tp", "group"),
+        P("group", "tp"),
+        P("group", "tp", None),
+        P("group", "tp", None),
+        P("group"),
+    )
+    out_specs = P("group", None, "tp")
+    return jax.shard_map(local, mesh=mesh, in_specs=in_specs, out_specs=out_specs, check_vma=False)

time: 86.4 us -> 84.5 us (0.978)
  the two profiles are of different devices: /device:TPU:2 before, /device:TPU:40 now
where the time goes in v4:
time: 84.5 us; the launch traced here: 84 us
  blocking collectives  30.9 us (37%)
  starting transfers between devices  24 us (28%)
  waiting for transfers between devices  13.7 us (16%)
  Pallas kernels  13.3 us (16%)
  local copies, waits for them, and re-layouts  2.03 us (2%)
    all_to_all x2, blocking collectives, swap(): return lax.all_to_all(block, axis, 0, 0)  30.9 us
    all_to_all x3, starting transfers between devices, swap(): return lax.all_to_all(block, axis, 0, 0)  20.1 us
    pallas_call x10, Pallas kernels, call(): pl.pallas_call(body, out_shape=out_shapes, in_specs=specs, out_specs=tupl...  13.3 us
    all_to_all x3, waiting for transfers between devices, swap(): return lax.all_to_all(block, axis, 0, 0)  10.9 us
    ppermute x3, starting transfers between devices, local(): lax.ppermute(near, 'tp', [(i, i ^ k) for i in range(PARTS)])  3.83 us
    ppermute x3, waiting for transfers between devices, local(): lax.ppermute(near, 'tp', [(i, i ^ k) for i in range(PARTS)])  2.74 us
    unnamed x16, local copies, waits for them, and re-layouts  2.03 us
  transfers between devices with their start and end apart: 6, of which 5 were waited for; matrix products, arithmetic and copies ran while one was open for 0% of the time, Pallas kernels for 7%

profile of v4, /device:TPU:40, one launch (start us, length us, event | category | flops | bytes accessed | tf_op | source)
XLA Modules:
  0.0 84.0 jit_solution(6701310892432448218)
XLA Ops:
  0.0 1.6 %shard_map.172 = bf16[16,24,384]{2,1,0:T(8,128)(2,1)} custom-call(bf16[12,320]{1,0:T(8,128)(2,1)} %bitcast.7, bf16[4,256]{1,0:T(4,128)(2,1)} %bitcast.8, bf16[4,256]{1,0:T(4,128)(2,1)} %refs_2_.1, bf16[4,32]{1,0:T(4,128)(2,1)} %refs_3_.1, bf16[4,32]{1,0:T(4,128)(2,1)} %refs_4_.1, bf16[4,320]{1,0:T(4,128)(2,1)} %refs_5_.1), custom_call_target="tpu_custom_call" | custom-call | tf_op jit(solution)/shard_map/pallas_call | solution.py:34
  1.6 0.0 copy-start.5
  1.6 6.1 %all-to-all-start = ((bf16[16,24,384]{2,1,0:T(8,128)(2,1)}), bf16[16,24,384]{2,1,0:T(8,128)(2,1)S(1)}, u32[]{:S(2)}, u32[]{:S(2)}) async-start(bf16[16,24,384]{2,1,0:T(8,128)(2,1)} %shard_map.172), calls=%async_computation | async-start | bytes 589824 | tf_op jit(solution)/shard_map/all_to_all | solution.py:310
  7.8 0.0 copy-start.2
  7.8 0.7 copy-done.2
  8.5 0.7 copy-done.3
  9.1 0.7 copy-done.7
  9.8 3.3 %shard_map.173 = (bf16[32,5120]{1,0:T(8,128)(2,1)S(1)}, f32[32,128]{1,0:T(8,128)S(1)}, f32[32,128]{1,0:T(8,128)S(1)}, f32[32,256]{1,0:T(8,128)S(1)}, f32[32,128]{1,0:T(8,128)S(1)}) custom-call(s32[8]{0:T(128)S(1)} %copy-done.3, bf16[8,4,5120]{2,1,0:T(4,128)(2,1)} %x_any.1, bf16[5120]{0:T(1024)(128)(2,1)S(1)} %copy-done.2, f32[1,128]{1,0:T(1,128)S(1)} %copy-done.7, ...), custom_call_target="tpu_custom_call" | custom-call | bytes 16777216 | tf_op jit(solution)/shard_map/pallas_call | solution.py:34
  13.2 4.3 %all-to-all-done.packed = bf16[16,24,384]{2,1,0:T(8,128)(2,1)S(1)} async-done(((bf16[16,24,384]{2,1,0:T(8,128)(2,1)}), bf16[16,24,384]{2,1,0:T(8,128)(2,1)S(1)}, u32[]{:S(2)}, u32[]{:S(2)}) %all-to-all-start) | async-done | bytes 294944 | tf_op jit(solution)/shard_map/all_to_all | solution.py:310
  17.5 0.9 %shard_map.174 = (bf16[16,16,128]{2,1,0:T(8,128)(2,1)}, bf16[48,128]{1,0:T(8,128)(2,1)S(1)}) custom-call(bf16[16,24,384]{2,1,0:T(8,128)(2,1)S(1)} %all-to-all-done.packed, bf16[32,5120]{1,0:T(8,128)(2,1)S(1)} %get-tuple-element.31.normed, f32[32,128]{1,0:T(8,128)S(1)} %get-tuple-element.32.fresh), custom_call_target="tpu_custom_call" | custom-call | tf_op jit(solution)/shard_map/pallas_call | solution.py:34
  18.4 9.5 %all-to-all-start.1 = ((bf16[16,16,128]{2,1,0:T(8,128)(2,1)}), bf16[16,16,128]{2,1,0:T(8,128)(2,1)S(1)}, u32[]{:S(2)}, u32[]{:S(2)}) async-start(bf16[16,16,128]{2,1,0:T(8,128)(2,1)} %get-tuple-element.33), calls=%async_computation.1 | async-start | bytes 131072 | tf_op jit(solution)/shard_map/all_to_all | solution.py:310
  27.9 1.5 %collective-permute-start.2 = (bf16[48,128]{1,0:T(8,128)(2,1)S(1)}, bf16[48,128]{1,0:T(8,128)(2,1)S(1)}, u32[]{:S(2)}, u32[]{:S(2)}) collective-permute-start(bf16[48,128]{1,0:T(8,128)(2,1)S(1)} %get-tuple-element.43.near), channel_id=1, source_target_pairs={{0,3},{1,2},{2,1},{3,0},{4,7},{5,6},{6,5},{7,4},{8,11},{9,10},{10,... | collective-permute-start | bytes 36872 | tf_op jit(solution)/shard_map/ppermute | solution.py:396
  29.3 1.5 %collective-permute-start.1 = (bf16[48,128]{1,0:T(8,128)(2,1)S(1)}, bf16[48,128]{1,0:T(8,128)(2,1)S(1)}, u32[]{:S(2)}, u32[]{:S(2)}) collective-permute-start(bf16[48,128]{1,0:T(8,128)(2,1)S(1)} %get-tuple-element.43.near), channel_id=1, source_target_pairs={{0,2},{1,3},{2,0},{3,1},{4,6},{5,7},{6,4},{7,5},{8,10},{9,11},{10,... | collective-permute-start | bytes 36872 | tf_op jit(solution)/shard_map/ppermute | solution.py:396
  30.8 0.9 %collective-permute-start = (bf16[48,128]{1,0:T(8,128)(2,1)S(1)}, bf16[48,128]{1,0:T(8,128)(2,1)S(1)}, u32[]{:S(2)}, u32[]{:S(2)}) collective-permute-start(bf16[48,128]{1,0:T(8,128)(2,1)S(1)} %get-tuple-element.43.near), channel_id=1, source_target_pairs={{0,1},{1,0},{2,3},{3,2},{4,5},{5,4},{6,7},{7,6},{8,9},{9,8},{10,11... | collective-permute-start | bytes 36872 | tf_op jit(solution)/shard_map/ppermute | solution.py:396
  31.7 0.0 collective-permute-done.2.near_3
  31.8 2.2 %collective-permute-done.1.near_2 = bf16[48,128]{1,0:T(8,128)(2,1)S(1)} collective-permute-done((bf16[48,128]{1,0:T(8,128)(2,1)S(1)}, bf16[48,128]{1,0:T(8,128)(2,1)S(1)}, u32[]{:S(2)}, u32[]{:S(2)}) %collective-permute-start.1) | collective-permute-done | bytes 12320 | tf_op jit(solution)/shard_map/ppermute | solution.py:396
  33.9 0.6 collective-permute-done.near_1
  34.5 0.2 all-to-all-done.1.low
  34.7 0.0 copy-done.5
  34.7 0.5 shard_map.176
  35.2 16.5 %all_to_all.25.gathered = bf16[16,64,128]{2,1,0:T(8,128)(2,1)S(1)} all-to-all(bf16[16,64,128]{2,1,0:T(8,128)(2,1)S(1)} %get-tuple-element.40), channel_id=1, replica_groups=mesh['group'=16,'tp'=16] {'tp'}, dimensions={0} | all-to-all | bytes 524288 | tf_op jit(solution)/shard_map/all_to_all | solution.py:310
  51.6 0.0 copy-done
  51.7 0.0 copy-done.1
  51.7 0.0 copy-done.4
  51.7 2.4 %shard_map.177 = bf16[16,72,128]{2,1,0:T(8,128)(2,1)} custom-call(s32[1]{0:T(128)} %bitcast.2.place, s32[8]{0:T(128)S(1)} %copy-done.4, bf16[16,64,128]{2,1,0:T(8,128)(2,1)S(1)} %all_to_all.25.gathered, bf16[8,128,512]{2,1,0:T(8,128)(2,1)S(1)} %copy-done, bf16[8,128,512]{2,1,0:T(8,128)(2,1)S(1)} %copy-done.1), custom_call_target="tpu_custom_call" | custom-call | tf_op jit(solution)/shard_map/pallas_call | solution.py:34
  54.1 4.5 %all-to-all-start.3 = ((bf16[16,72,128]{2,1,0:T(8,128)(2,1)}), bf16[16,72,128]{2,1,0:T(8,128)(2,1)S(1)}, u32[]{:S(2)}, u32[]{:S(2)}) async-start(bf16[16,72,128]{2,1,0:T(8,128)(2,1)} %shard_map.177), calls=%async_computation.3 | async-start | bytes 589824 | tf_op jit(solution)/shard_map/all_to_all | solution.py:310
  58.6 1.8 %shard_map.179.output_w = bf16[256,5120]{1,0:T(8,128)(2,1)S(1)} custom-call(bf16[256,5120]{1,0:T(8,128)(2,1)} %source), custom_call_target="tpu_custom_call" | custom-call | bytes 16777216 | tf_op jit(solution)/shard_map/pallas_call | solution.py:34
  60.4 0.8 shard_map.178
  61.2 6.4 %all-to-all-done.3.gathered = bf16[16,72,128]{2,1,0:T(8,128)(2,1)S(1)} async-done(((bf16[16,72,128]{2,1,0:T(8,128)(2,1)}), bf16[16,72,128]{2,1,0:T(8,128)(2,1)S(1)}, u32[]{:S(2)}, u32[]{:S(2)}) %all-to-all-start.3) | async-done | bytes 294944 | tf_op jit(solution)/shard_map/all_to_all | solution.py:310
  67.6 1.1 %shard_map.180 = bf16[16,32,384]{2,1,0:T(8,128)(2,1)S(1)} custom-call(bf16[16,72,128]{2,1,0:T(8,128)(2,1)S(1)} %all-to-all-done.3.gathered, f32[64,128]{1,0:T(8,128)S(1)} %get-tuple-element.48.own_weighted, f32[8,128]{1,0:T(8,128)S(1)} %get-tuple-element.49.own_stats, bf16[256,5120]{1,0:T(8,128)(2,1)S(1)} %shard_map.179.output_w, ...), custom_call_target="tpu_custom_call" | custom-call | tf_op jit(solution)/shard_map/pallas_call | solution.py:34
  68.7 14.4 %all_to_all.26.gathered = bf16[16,32,384]{2,1,0:T(8,128)(2,1)S(1)} all-to-all(bf16[16,32,384]{2,1,0:T(8,128)(2,1)S(1)} %shard_map.180), channel_id=1, replica_groups=mesh['group'=16,'tp'=16] {'tp'}, dimensions={0} | all-to-all | bytes 786432 | tf_op jit(solution)/shard_map/all_to_all | solution.py:310
  83.1 0.8 shard_map.181
  (8 shorter events, 0.0 us)
Async XLA Ops:
  1.6 33.1 %copy-start.5 = (bf16[128]{0:T(256)(128)(2,1)S(1)}, bf16[128]{0:T(256)(128)(2,1)}, u32[]{:S(2)}) copy-start(bf16[128]{0:T(256)(128)(2,1)} %gain.2) | copy-start | bytes 772
  1.6 15.9 %all-to-all-start = ((bf16[16,24,384]{2,1,0:T(8,128)(2,1)}), bf16[16,24,384]{2,1,0:T(8,128)(2,1)S(1)}, u32[]{:S(2)}, u32[]{:S(2)}) async-start(bf16[16,24,384]{2,1,0:T(8,128)(2,1)} %shard_map.172), calls=%async_computation | async-start | bytes 589824 | tf_op jit(solution)/shard_map/all_to_all | solution.py:310
  7.8 0.7 copy-start.2
  8.5 0.7 copy-start.3
  9.1 0.7 copy-start.7
  9.8 41.9 %copy-start = (bf16[8,128,512]{2,1,0:T(8,128)(2,1)S(1)}, bf16[8,128,512]{2,1,0:T(8,128)(2,1)}, u32[]{:S(2)}) copy-start(bf16[8,128,512]{2,1,0:T(8,128)(2,1)} %keys.1) | copy-start | bytes 3145732
  9.8 41.9 %copy-start.1 = (bf16[8,128,512]{2,1,0:T(8,128)(2,1)S(1)}, bf16[8,128,512]{2,1,0:T(8,128)(2,1)}, u32[]{:S(2)}) copy-start(bf16[8,128,512]{2,1,0:T(8,128)(2,1)} %values.1) | copy-start | bytes 3145732
  9.8 41.9 %copy-start.4 = (s32[8]{0:T(128)S(1)}, s32[8]{0:T(128)}, u32[]{:S(2)}) copy-start(s32[8]{0:T(128)} %lengths.3) | copy-start | bytes 100
  18.4 16.3 %all-to-all-start.1 = ((bf16[16,16,128]{2,1,0:T(8,128)(2,1)}), bf16[16,16,128]{2,1,0:T(8,128)(2,1)S(1)}, u32[]{:S(2)}, u32[]{:S(2)}) async-start(bf16[16,16,128]{2,1,0:T(8,128)(2,1)} %get-tuple-element.33), calls=%async_computation.1 | async-start | bytes 131072 | tf_op jit(solution)/shard_map/all_to_all | solution.py:310
  27.9 3.9 %collective-permute-start.2 = (bf16[48,128]{1,0:T(8,128)(2,1)S(1)}, bf16[48,128]{1,0:T(8,128)(2,1)S(1)}, u32[]{:S(2)}, u32[]{:S(2)}) collective-permute-start(bf16[48,128]{1,0:T(8,128)(2,1)S(1)} %get-tuple-element.43.near), channel_id=1, source_target_pairs={{0,3},{1,2},{2,1},{3,0},{4,7},{5,6},{6,5},{7,4},{8,11},{9,10},{10,... | collective-permute-start | bytes 36872 | tf_op jit(solution)/shard_map/ppermute | solution.py:396
  29.3 4.6 %collective-permute-start.1 = (bf16[48,128]{1,0:T(8,128)(2,1)S(1)}, bf16[48,128]{1,0:T(8,128)(2,1)S(1)}, u32[]{:S(2)}, u32[]{:S(2)}) collective-permute-start(bf16[48,128]{1,0:T(8,128)(2,1)S(1)} %get-tuple-element.43.near), channel_id=1, source_target_pairs={{0,2},{1,3},{2,0},{3,1},{4,6},{5,7},{6,4},{7,5},{8,10},{9,11},{10,... | collective-permute-start | bytes 36872 | tf_op jit(solution)/shard_map/ppermute | solution.py:396
  30.8 3.7 %collective-permute-start = (bf16[48,128]{1,0:T(8,128)(2,1)S(1)}, bf16[48,128]{1,0:T(8,128)(2,1)S(1)}, u32[]{:S(2)}, u32[]{:S(2)}) collective-permute-start(bf16[48,128]{1,0:T(8,128)(2,1)S(1)} %get-tuple-element.43.near), channel_id=1, source_target_pairs={{0,1},{1,0},{2,3},{3,2},{4,5},{5,4},{6,7},{7,6},{8,9},{9,8},{10,11... | collective-permute-start | bytes 36872 | tf_op jit(solution)/shard_map/ppermute | solution.py:396
  54.1 13.5 %all-to-all-start.3 = ((bf16[16,72,128]{2,1,0:T(8,128)(2,1)}), bf16[16,72,128]{2,1,0:T(8,128)(2,1)S(1)}, u32[]{:S(2)}, u32[]{:S(2)}) async-start(bf16[16,72,128]{2,1,0:T(8,128)(2,1)} %shard_map.177), calls=%async_computation.3 | async-start | bytes 589824 | tf_op jit(solution)/shard_map/all_to_all | solution.py:310
  58.6 1.8 %copy-start.6 = (bf16[128]{0:T(256)(128)(2,1)S(1)}, bf16[128]{0:T(256)(128)(2,1)}, u32[]{:S(2)}) copy-start(bf16[128]{0:T(256)(128)(2,1)} %gain.3) | copy-start | bytes 772

commit v5 on v4

--- a/solution.py
+++ b/solution.py
@@ -138,15 +138,9 @@
     near[16:48] = fold(lift).astype(BF16)
 
 
-def unpack_body(packed, ups, out_down, out_up):
+def unpack_body(packed, out_down, out_up):
     pieces = [packed[g].astype(F32) for g in range(GROUPS)]
     out_down[...] = jnp.concatenate([p[12:16, 0:256] for p in pieces], axis=0).astype(BF16)
-    lift = jnp.concatenate([p[16:20, 0:256] for p in pieces], axis=0)
-    lift = jnp.concatenate([lift, jnp.zeros((8, 256), F32)], axis=0)
-    rest = jnp.zeros((4, 256), F32)
-    for t in range(6):
-        block = jnp.concatenate([lift[t * 12 : (t + 1) * 12], rest], axis=0)
-        ups[t * 16 : (t + 1) * 16] = block.astype(BF16)
     out_up[...] = jnp.concatenate([p[20:24] for p in pieces], axis=0).astype(BF16)
 
 
@@ -163,9 +157,11 @@
     return jnp.where(col == source, 1.0, 0.0).astype(BF16)
 
 
-def query_body(low, base, ups, cosines, sines, gain, packed, own):
-    ranks = low[0:6].reshape(96, 128)[:, 0:32]
-    update = dot(ranks, ups[...], (0, 0))
+def query_body(low, packed, base, cosines, sines, gain, sent, own):
+    ranks = jnp.concatenate([low[t].astype(F32)[0:12] for t in range(6)], axis=0)
+    ranks = ranks[0:64, 0:32].astype(BF16)
+    lift = [packed[g].astype(F32)[16:20, 0:256] for g in range(GROUPS)]
+    update = dot(ranks, jnp.concatenate(lift, axis=0).astype(BF16), (0, 0))
     raw = base[...] + ADAPTER_SCALE * update
     scale = gain[...].astype(F32).reshape(1, -1)
     heads = [
@@ -175,7 +171,7 @@
     queries = jnp.concatenate(heads, axis=0).astype(BF16)
     queries = dot(regroup(8, 2), queries).astype(BF16)
     for i in range(PARTS):
-        packed[i] = queries
+        sent[i] = queries
     own[...] = queries
 
 
@@ -395,19 +391,11 @@
     near = [near] + [
         lax.ppermute(near, "tp", [(i, i ^ k) for i in range(PARTS)]) for k in range(1, 4)
     ]
-    ups, out_down, out_up = call(
-        unpack_body,
-        (SHAPE((96, 256), BF16), SHAPE((64, 256), BF16), SHAPE((64, 384), BF16)),
-        (packed,),
-        "v",
-        20,
-        moved=WINDOW,
-    )
     low, near = lax.optimization_barrier((low, near))
     queries, own = call(
         query_body,
         (SHAPE((PARTS, 64, 128), BF16), SHAPE((64, 128), BF16)),
-        (low, base, ups, cosines, sines, query_norm_gain),
+        (low, packed, base, cosines, sines, query_norm_gain),
         "vvvvvv",
         20,
     )
@@ -419,10 +407,20 @@
         "ssvvv",
         20,
     )
-    parts, own, output_late = lax.optimization_barrier((parts, own, output_matrix))
+    parts, own, output_late, late = lax.optimization_barrier(
+        (parts, own, output_matrix, packed)
+    )
     parts = swap(parts, "tp")
     output_late = call(
         load_body, SHAPE(output_matrix.shape, BF16), (output_late,), "a", 14, [dma], moved=WINDOW
+    )
+    out_down, out_up = call(
+        unpack_body,
+        (SHAPE((64, 256), BF16), SHAPE((64, 384), BF16)),
+        (late,),
+        "v",
+        20,
+        moved=WINDOW,
     )
     own_weighted, own_stats = call(
         fresh_body,

time: 84.5 us -> 84.5 us (level)
  no operation moved by 1% of the time
where the time goes in v5:
time: 84.5 us; the launch traced here: 84 us
  blocking collectives  30.9 us (37%)
  starting transfers between devices  24 us (28%)
  waiting for transfers between devices  13.7 us (16%)
  Pallas kernels  13.3 us (16%)
  local copies, waits for them, and re-layouts  2.03 us (2%)
    all_to_all x2, blocking collectives, swap(): return lax.all_to_all(block, axis, 0, 0)  30.9 us
    all_to_all x3, starting transfers between devices, swap(): return lax.all_to_all(block, axis, 0, 0)  20.1 us
    pallas_call x10, Pallas kernels, call(): pl.pallas_call(body, out_shape=out_shapes, in_specs=specs, out_specs=tupl...  13.3 us
    all_to_all x3, waiting for transfers between devices, swap(): return lax.all_to_all(block, axis, 0, 0)  10.9 us
    ppermute x3, starting transfers between devices, local(): lax.ppermute(near, 'tp', [(i, i ^ k) for i in range(PARTS)])  3.83 us
    ppermute x3, waiting for transfers between devices, local(): lax.ppermute(near, 'tp', [(i, i ^ k) for i in range(PARTS)])  2.79 us
    unnamed x16, local copies, waits for them, and re-layouts  2.03 us
  transfers between devices with their start and end apart: 6, of which 5 were waited for; matrix products, arithmetic and copies ran while one was open for 0% of the time, Pallas kernels for 7%

profile of v5, /device:TPU:40, one launch (start us, length us, event | category | flops | bytes accessed | tf_op | source)
XLA Modules:
  0.0 84.0 jit_solution(4016618942108476715)
XLA Ops:
  0.0 1.6 %shard_map.172 = bf16[16,24,384]{2,1,0:T(8,128)(2,1)} custom-call(bf16[12,320]{1,0:T(8,128)(2,1)} %bitcast.7, bf16[4,256]{1,0:T(4,128)(2,1)} %bitcast.8, bf16[4,256]{1,0:T(4,128)(2,1)} %refs_2_.1, bf16[4,32]{1,0:T(4,128)(2,1)} %refs_3_.1, bf16[4,32]{1,0:T(4,128)(2,1)} %refs_4_.1, bf16[4,320]{1,0:T(4,128)(2,1)} %refs_5_.1), custom_call_target="tpu_custom_call" | custom-call | tf_op jit(solution)/shard_map/pallas_call | solution.py:34
  1.6 6.1 %all-to-all-start = ((bf16[16,24,384]{2,1,0:T(8,128)(2,1)}), bf16[16,24,384]{2,1,0:T(8,128)(2,1)S(1)}, u32[]{:S(2)}, u32[]{:S(2)}) async-start(bf16[16,24,384]{2,1,0:T(8,128)(2,1)} %shard_map.172), calls=%async_computation | async-start | bytes 589824 | tf_op jit(solution)/shard_map/all_to_all | solution.py:306
  7.8 0.0 copy-start.2
  7.8 0.7 copy-done.2
  8.5 0.7 copy-done.3
  9.1 0.7 copy-done.7
  9.8 3.3 %shard_map.173 = (bf16[32,5120]{1,0:T(8,128)(2,1)S(1)}, f32[32,128]{1,0:T(8,128)S(1)}, f32[32,128]{1,0:T(8,128)S(1)}, f32[32,256]{1,0:T(8,128)S(1)}, f32[32,128]{1,0:T(8,128)S(1)}) custom-call(s32[8]{0:T(128)S(1)} %copy-done.3, bf16[8,4,5120]{2,1,0:T(4,128)(2,1)} %x_any.1, bf16[5120]{0:T(1024)(128)(2,1)S(1)} %copy-done.2, f32[1,128]{1,0:T(1,128)S(1)} %copy-done.7, ...), custom_call_target="tpu_custom_call" | custom-call | bytes 16777216 | tf_op jit(solution)/shard_map/pallas_call | solution.py:34
  13.2 4.3 %all-to-all-done.packed = bf16[16,24,384]{2,1,0:T(8,128)(2,1)S(1)} async-done(((bf16[16,24,384]{2,1,0:T(8,128)(2,1)}), bf16[16,24,384]{2,1,0:T(8,128)(2,1)S(1)}, u32[]{:S(2)}, u32[]{:S(2)}) %all-to-all-start) | async-done | bytes 294944 | tf_op jit(solution)/shard_map/all_to_all | solution.py:306
  17.5 0.9 %shard_map.174 = (bf16[16,16,128]{2,1,0:T(8,128)(2,1)}, bf16[48,128]{1,0:T(8,128)(2,1)S(1)}) custom-call(bf16[16,24,384]{2,1,0:T(8,128)(2,1)S(1)} %all-to-all-done.packed, bf16[32,5120]{1,0:T(8,128)(2,1)S(1)} %get-tuple-element.31.normed, f32[32,128]{1,0:T(8,128)S(1)} %get-tuple-element.32.fresh), custom_call_target="tpu_custom_call" | custom-call | tf_op jit(solution)/shard_map/pallas_call | solution.py:34
  18.4 9.5 %all-to-all-start.1 = ((bf16[16,16,128]{2,1,0:T(8,128)(2,1)}), bf16[16,16,128]{2,1,0:T(8,128)(2,1)S(1)}, u32[]{:S(2)}, u32[]{:S(2)}) async-start(bf16[16,16,128]{2,1,0:T(8,128)(2,1)} %get-tuple-element.33), calls=%async_computation.1 | async-start | bytes 131072 | tf_op jit(solution)/shard_map/all_to_all | solution.py:306
  27.9 1.5 %collective-permute-start.2 = (bf16[48,128]{1,0:T(8,128)(2,1)S(1)}, bf16[48,128]{1,0:T(8,128)(2,1)S(1)}, u32[]{:S(2)}, u32[]{:S(2)}) collective-permute-start(bf16[48,128]{1,0:T(8,128)(2,1)S(1)} %get-tuple-element.42.near), channel_id=1, source_target_pairs={{0,3},{1,2},{2,1},{3,0},{4,7},{5,6},{6,5},{7,4},{8,11},{9,10},{10,... | collective-permute-start | bytes 36872 | tf_op jit(solution)/shard_map/ppermute | solution.py:392
  29.3 1.5 %collective-permute-start.1 = (bf16[48,128]{1,0:T(8,128)(2,1)S(1)}, bf16[48,128]{1,0:T(8,128)(2,1)S(1)}, u32[]{:S(2)}, u32[]{:S(2)}) collective-permute-start(bf16[48,128]{1,0:T(8,128)(2,1)S(1)} %get-tuple-element.42.near), channel_id=1, source_target_pairs={{0,2},{1,3},{2,0},{3,1},{4,6},{5,7},{6,4},{7,5},{8,10},{9,11},{10,... | collective-permute-start | bytes 36872 | tf_op jit(solution)/shard_map/ppermute | solution.py:392
  30.8 0.9 %collective-permute-start = (bf16[48,128]{1,0:T(8,128)(2,1)S(1)}, bf16[48,128]{1,0:T(8,128)(2,1)S(1)}, u32[]{:S(2)}, u32[]{:S(2)}) collective-permute-start(bf16[48,128]{1,0:T(8,128)(2,1)S(1)} %get-tuple-element.42.near), channel_id=1, source_target_pairs={{0,1},{1,0},{2,3},{3,2},{4,5},{5,4},{6,7},{7,6},{8,9},{9,8},{10,11... | collective-permute-start | bytes 36872 | tf_op jit(solution)/shard_map/ppermute | solution.py:392
  31.7 0.0 collective-permute-done.2.near_3
  31.7 2.2 %collective-permute-done.1.near_2 = bf16[48,128]{1,0:T(8,128)(2,1)S(1)} collective-permute-done((bf16[48,128]{1,0:T(8,128)(2,1)S(1)}, bf16[48,128]{1,0:T(8,128)(2,1)S(1)}, u32[]{:S(2)}, u32[]{:S(2)}) %collective-permute-start.1) | collective-permute-done | bytes 12320 | tf_op jit(solution)/shard_map/ppermute | solution.py:392
  33.9 0.6 collective-permute-done.near_1
  34.5 0.2 all-to-all-done.1.low
  34.7 0.0 copy-done.5
  34.7 0.5 shard_map.175
  35.2 16.5 %all_to_all.25.gathered = bf16[16,64,128]{2,1,0:T(8,128)(2,1)S(1)} all-to-all(bf16[16,64,128]{2,1,0:T(8,128)(2,1)S(1)} %get-tuple-element.39), channel_id=1, replica_groups=mesh['group'=16,'tp'=16] {'tp'}, dimensions={0} | all-to-all | bytes 524288 | tf_op jit(solution)/shard_map/all_to_all | solution.py:306
  51.7 0.0 copy-done
  51.7 0.0 copy-done.1
  51.7 2.4 %shard_map.176 = bf16[16,72,128]{2,1,0:T(8,128)(2,1)} custom-call(s32[1]{0:T(128)} %bitcast.2.place, s32[8]{0:T(128)S(1)} %copy-done.4, bf16[16,64,128]{2,1,0:T(8,128)(2,1)S(1)} %all_to_all.25.gathered, bf16[8,128,512]{2,1,0:T(8,128)(2,1)S(1)} %copy-done, bf16[8,128,512]{2,1,0:T(8,128)(2,1)S(1)} %copy-done.1), custom_call_target="tpu_custom_call" | custom-call | tf_op jit(solution)/shard_map/pallas_call | solution.py:34
  54.1 4.5 %all-to-all-start.3 = ((bf16[16,72,128]{2,1,0:T(8,128)(2,1)}), bf16[16,72,128]{2,1,0:T(8,128)(2,1)S(1)}, u32[]{:S(2)}, u32[]{:S(2)}) async-start(bf16[16,72,128]{2,1,0:T(8,128)(2,1)} %shard_map.176), calls=%async_computation.3 | async-start | bytes 589824 | tf_op jit(solution)/shard_map/all_to_all | solution.py:306
  58.6 0.0 copy-start.6
  58.6 1.8 %shard_map.178.output_w = bf16[256,5120]{1,0:T(8,128)(2,1)S(1)} custom-call(bf16[256,5120]{1,0:T(8,128)(2,1)} %source), custom_call_target="tpu_custom_call" | custom-call | bytes 16777216 | tf_op jit(solution)/shard_map/pallas_call | solution.py:34
  60.4 0.0 copy-done.6
  60.4 0.8 shard_map.177
  61.2 6.4 %all-to-all-done.3.gathered = bf16[16,72,128]{2,1,0:T(8,128)(2,1)S(1)} async-done(((bf16[16,72,128]{2,1,0:T(8,128)(2,1)}), bf16[16,72,128]{2,1,0:T(8,128)(2,1)S(1)}, u32[]{:S(2)}, u32[]{:S(2)}) %all-to-all-start.3) | async-done | bytes 294944 | tf_op jit(solution)/shard_map/all_to_all | solution.py:306
  67.6 1.1 %shard_map.180 = bf16[16,32,384]{2,1,0:T(8,128)(2,1)S(1)} custom-call(bf16[16,72,128]{2,1,0:T(8,128)(2,1)S(1)} %all-to-all-done.3.gathered, f32[64,128]{1,0:T(8,128)S(1)} %get-tuple-element.47.own_weighted, f32[8,128]{1,0:T(8,128)S(1)} %get-tuple-element.48.own_stats, bf16[256,5120]{1,0:T(8,128)(2,1)S(1)} %shard_map.178.output_w, ...), custom_call_target="tpu_custom_call" | custom-call | tf_op jit(solution)/shard_map/pallas_call | solution.py:34
  68.7 14.4 %all_to_all.26.gathered = bf16[16,32,384]{2,1,0:T(8,128)(2,1)S(1)} all-to-all(bf16[16,32,384]{2,1,0:T(8,128)(2,1)S(1)} %shard_map.180), channel_id=1, replica_groups=mesh['group'=16,'tp'=16] {'tp'}, dimensions={0} | all-to-all | bytes 786432 | tf_op jit(solution)/shard_map/all_to_all | solution.py:306
  83.1 0.8 shard_map.181
  (8 shorter events, 0.0 us)
Async XLA Ops:
  0.0 34.7 %copy-start.5 = (bf16[128]{0:T(256)(128)(2,1)S(1)}, bf16[128]{0:T(256)(128)(2,1)}, u32[]{:S(2)}) copy-start(bf16[128]{0:T(256)(128)(2,1)} %gain.2) | copy-start | bytes 772
  1.6 15.9 %all-to-all-start = ((bf16[16,24,384]{2,1,0:T(8,128)(2,1)}), bf16[16,24,384]{2,1,0:T(8,128)(2,1)S(1)}, u32[]{:S(2)}, u32[]{:S(2)}) async-start(bf16[16,24,384]{2,1,0:T(8,128)(2,1)} %shard_map.172), calls=%async_computation | async-start | bytes 589824 | tf_op jit(solution)/shard_map/all_to_all | solution.py:306
  7.8 0.7 copy-start.2
  8.5 0.7 copy-start.3
  9.1 0.7 copy-start.7
  9.8 41.9 %copy-start = (bf16[8,128,512]{2,1,0:T(8,128)(2,1)S(1)}, bf16[8,128,512]{2,1,0:T(8,128)(2,1)}, u32[]{:S(2)}) copy-start(bf16[8,128,512]{2,1,0:T(8,128)(2,1)} %keys.1) | copy-start | bytes 3145732
  9.8 41.9 %copy-start.1 = (bf16[8,128,512]{2,1,0:T(8,128)(2,1)S(1)}, bf16[8,128,512]{2,1,0:T(8,128)(2,1)}, u32[]{:S(2)}) copy-start(bf16[8,128,512]{2,1,0:T(8,128)(2,1)} %values.1) | copy-start | bytes 3145732
  9.8 41.9 %copy-start.4 = (s32[8]{0:T(128)S(1)}, s32[8]{0:T(128)}, u32[]{:S(2)}) copy-start(s32[8]{0:T(128)} %lengths.3) | copy-start | bytes 100
  18.4 16.3 %all-to-all-start.1 = ((bf16[16,16,128]{2,1,0:T(8,128)(2,1)}), bf16[16,16,128]{2,1,0:T(8,128)(2,1)S(1)}, u32[]{:S(2)}, u32[]{:S(2)}) async-start(bf16[16,16,128]{2,1,0:T(8,128)(2,1)} %get-tuple-element.33), calls=%async_computation.1 | async-start | bytes 131072 | tf_op jit(solution)/shard_map/all_to_all | solution.py:306
  27.9 3.8 %collective-permute-start.2 = (bf16[48,128]{1,0:T(8,128)(2,1)S(1)}, bf16[48,128]{1,0:T(8,128)(2,1)S(1)}, u32[]{:S(2)}, u32[]{:S(2)}) collective-permute-start(bf16[48,128]{1,0:T(8,128)(2,1)S(1)} %get-tuple-element.42.near), channel_id=1, source_target_pairs={{0,3},{1,2},{2,1},{3,0},{4,7},{5,6},{6,5},{7,4},{8,11},{9,10},{10,... | collective-permute-start | bytes 36872 | tf_op jit(solution)/shard_map/ppermute | solution.py:392
  29.3 4.6 %collective-permute-start.1 = (bf16[48,128]{1,0:T(8,128)(2,1)S(1)}, bf16[48,128]{1,0:T(8,128)(2,1)S(1)}, u32[]{:S(2)}, u32[]{:S(2)}) collective-permute-start(bf16[48,128]{1,0:T(8,128)(2,1)S(1)} %get-tuple-element.42.near), channel_id=1, source_target_pairs={{0,2},{1,3},{2,0},{3,1},{4,6},{5,7},{6,4},{7,5},{8,10},{9,11},{10,... | collective-permute-start | bytes 36872 | tf_op jit(solution)/shard_map/ppermute | solution.py:392
  30.8 3.7 %collective-permute-start = (bf16[48,128]{1,0:T(8,128)(2,1)S(1)}, bf16[48,128]{1,0:T(8,128)(2,1)S(1)}, u32[]{:S(2)}, u32[]{:S(2)}) collective-permute-start(bf16[48,128]{1,0:T(8,128)(2,1)S(1)} %get-tuple-element.42.near), channel_id=1, source_target_pairs={{0,1},{1,0},{2,3},{3,2},{4,5},{5,4},{6,7},{7,6},{8,9},{9,8},{10,11... | collective-permute-start | bytes 36872 | tf_op jit(solution)/shard_map/ppermute | solution.py:392
  54.1 13.5 %all-to-all-start.3 = ((bf16[16,72,128]{2,1,0:T(8,128)(2,1)}), bf16[16,72,128]{2,1,0:T(8,128)(2,1)S(1)}, u32[]{:S(2)}, u32[]{:S(2)}) async-start(bf16[16,72,128]{2,1,0:T(8,128)(2,1)} %shard_map.176), calls=%async_computation.3 | async-start | bytes 589824 | tf_op jit(solution)/shard_map/all_to_all | solution.py:306
  58.6 1.8 %copy-start.6 = (bf16[128]{0:T(256)(128)(2,1)S(1)}, bf16[128]{0:T(256)(128)(2,1)}, u32[]{:S(2)}) copy-start(bf16[128]{0:T(256)(128)(2,1)} %gain.3) | copy-start | bytes 772

commit v6 on v5

--- a/solution.py
+++ b/solution.py
@@ -391,7 +391,6 @@
     near = [near] + [
         lax.ppermute(near, "tp", [(i, i ^ k) for i in range(PARTS)]) for k in range(1, 4)
     ]
-    low, near = lax.optimization_barrier((low, near))
     queries, own = call(
         query_body,
         (SHAPE((PARTS, 64, 128), BF16), SHAPE((64, 128), BF16)),

time: 84.5 us -> 84.7 us (level)
  the two profiles are of different devices: /device:TPU:40 before, /device:TPU:2 now
where the time goes in v6:
time: 84.7 us; the launch traced here: 84.2 us
  blocking collectives  47.4 us (56%)
  starting transfers between devices  16.5 us (19%)
  Pallas kernels  12.7 us (15%)
  waiting for transfers between devices  5.44 us (6%)
  local copies, waits for them, and re-layouts  2.03 us (2%)
    all_to_all x3, blocking collectives, swap(): return lax.all_to_all(block, axis, 0, 0)  47.4 us
    pallas_call x10, Pallas kernels, call(): pl.pallas_call(body, out_shape=out_shapes, in_specs=specs, out_specs=tupl...  12.7 us
    all_to_all x2, starting transfers between devices, swap(): return lax.all_to_all(block, axis, 0, 0)  12 us
    ppermute x3, starting transfers between devices, local(): lax.ppermute(near, 'tp', [(i, i ^ k) for i in range(PARTS)])  4.47 us
    ppermute x3, waiting for transfers between devices, local(): lax.ppermute(near, 'tp', [(i, i ^ k) for i in range(PARTS)])  3.22 us
    all_to_all x2, waiting for transfers between devices, swap(): return lax.all_to_all(block, axis, 0, 0)  2.22 us
    unnamed x16, local copies, waits for them, and re-layouts  2.03 us
  transfers between devices with their start and end apart: 5, of which 3 were waited for; matrix products, arithmetic and copies ran while one was open for 0% of the time, Pallas kernels for 7%

profile of v6, /device:TPU:2, one launch (start us, length us, event | category | flops | bytes accessed | tf_op | source)
XLA Modules:
  0.0 84.2 jit_solution(10708485924170220535)
XLA Ops:
  0.0 0.0 copy-start.5
  0.0 1.6 %shard_map.172 = bf16[16,24,384]{2,1,0:T(8,128)(2,1)} custom-call(bf16[12,320]{1,0:T(8,128)(2,1)} %bitcast.7, bf16[4,256]{1,0:T(4,128)(2,1)} %bitcast.8, bf16[4,256]{1,0:T(4,128)(2,1)} %refs_2_.1, bf16[4,32]{1,0:T(4,128)(2,1)} %refs_3_.1, bf16[4,32]{1,0:T(4,128)(2,1)} %refs_4_.1, bf16[4,320]{1,0:T(4,128)(2,1)} %refs_5_.1), custom_call_target="tpu_custom_call" | custom-call | tf_op jit(solution)/shard_map/pallas_call | solution.py:34
  1.6 7.5 %all-to-all-start = ((bf16[16,24,384]{2,1,0:T(8,128)(2,1)}), bf16[16,24,384]{2,1,0:T(8,128)(2,1)S(1)}, u32[]{:S(2)}, u32[]{:S(2)}) async-start(bf16[16,24,384]{2,1,0:T(8,128)(2,1)} %shard_map.172), calls=%async_computation | async-start | bytes 589824 | tf_op jit(solution)/shard_map/all_to_all | solution.py:306
  9.1 0.7 copy-done.2
  9.8 0.7 copy-done.3
  10.5 0.7 copy-done.7
  11.1 3.3 %shard_map.173 = (bf16[32,5120]{1,0:T(8,128)(2,1)S(1)}, f32[32,128]{1,0:T(8,128)S(1)}, f32[32,128]{1,0:T(8,128)S(1)}, f32[32,256]{1,0:T(8,128)S(1)}, f32[32,128]{1,0:T(8,128)S(1)}) custom-call(s32[8]{0:T(128)S(1)} %copy-done.3, bf16[8,4,5120]{2,1,0:T(4,128)(2,1)} %x_any.1, bf16[5120]{0:T(1024)(128)(2,1)S(1)} %copy-done.2, f32[1,128]{1,0:T(1,128)S(1)} %copy-done.7, ...), custom_call_target="tpu_custom_call" | custom-call | bytes 16777216 | tf_op jit(solution)/shard_map/pallas_call | solution.py:34
  14.5 1.8 %all-to-all-done.packed = bf16[16,24,384]{2,1,0:T(8,128)(2,1)S(1)} async-done(((bf16[16,24,384]{2,1,0:T(8,128)(2,1)}), bf16[16,24,384]{2,1,0:T(8,128)(2,1)S(1)}, u32[]{:S(2)}, u32[]{:S(2)}) %all-to-all-start) | async-done | bytes 294944 | tf_op jit(solution)/shard_map/all_to_all | solution.py:306
  16.3 0.3 shard_map.174
  16.6 17.1 %all_to_all.25.low = bf16[16,16,128]{2,1,0:T(8,128)(2,1)S(1)} all-to-all(bf16[16,16,128]{2,1,0:T(8,128)(2,1)S(1)} %get-tuple-element.28), channel_id=1, replica_groups=mesh['group'=16,'tp'=16] {'tp'}, dimensions={0} | all-to-all | bytes 131072 | tf_op jit(solution)/shard_map/all_to_all | solution.py:306
  33.6 0.0 copy-done.5
  33.7 0.5 shard_map.175
  34.1 12.6 %all_to_all.26.gathered = bf16[16,64,128]{2,1,0:T(8,128)(2,1)S(1)} all-to-all(bf16[16,64,128]{2,1,0:T(8,128)(2,1)S(1)} %get-tuple-element.32), channel_id=1, replica_groups=mesh['group'=16,'tp'=16] {'tp'}, dimensions={0} | all-to-all | bytes 524288 | tf_op jit(solution)/shard_map/all_to_all | solution.py:306
  46.7 0.0 copy-done
  46.7 0.0 copy-done.1
  46.7 0.0 copy-done.4
  46.7 2.4 %shard_map.176 = bf16[16,72,128]{2,1,0:T(8,128)(2,1)} custom-call(s32[1]{0:T(128)} %bitcast.2.place, s32[8]{0:T(128)S(1)} %copy-done.4, bf16[16,64,128]{2,1,0:T(8,128)(2,1)S(1)} %all_to_all.26.gathered, bf16[8,128,512]{2,1,0:T(8,128)(2,1)S(1)} %copy-done, bf16[8,128,512]{2,1,0:T(8,128)(2,1)S(1)} %copy-done.1), custom_call_target="tpu_custom_call" | custom-call | tf_op jit(solution)/shard_map/pallas_call | solution.py:34
  49.1 4.6 %all-to-all-start.3 = ((bf16[16,72,128]{2,1,0:T(8,128)(2,1)}), bf16[16,72,128]{2,1,0:T(8,128)(2,1)S(1)}, u32[]{:S(2)}, u32[]{:S(2)}) async-start(bf16[16,72,128]{2,1,0:T(8,128)(2,1)} %shard_map.176), calls=%async_computation.3 | async-start | bytes 589824 | tf_op jit(solution)/shard_map/all_to_all | solution.py:306
  53.7 3.7 %collective-permute-start.2 = (bf16[48,128]{1,0:T(8,128)(2,1)S(1)}, bf16[48,128]{1,0:T(8,128)(2,1)S(1)}, u32[]{:S(2)}, u32[]{:S(2)}) collective-permute-start(bf16[48,128]{1,0:T(8,128)(2,1)S(1)} %get-tuple-element.35.near), channel_id=1, source_target_pairs={{0,3},{1,2},{2,1},{3,0},{4,7},{5,6},{6,5},{7,4},{8,11},{9,10},{10,... | collective-permute-start | bytes 36872 | tf_op jit(solution)/shard_map/ppermute | solution.py:392
  57.4 0.0 collective-permute-start.1
  57.4 0.7 collective-permute-start
  58.2 0.0 copy-start.6
  58.2 1.8 %shard_map.178.output_w = bf16[256,5120]{1,0:T(8,128)(2,1)S(1)} custom-call(bf16[256,5120]{1,0:T(8,128)(2,1)} %source), custom_call_target="tpu_custom_call" | custom-call | bytes 16777216 | tf_op jit(solution)/shard_map/pallas_call | solution.py:34
  60.0 3.2 %collective-permute-done.2.near_3 = bf16[48,128]{1,0:T(8,128)(2,1)S(1)} collective-permute-done((bf16[48,128]{1,0:T(8,128)(2,1)S(1)}, bf16[48,128]{1,0:T(8,128)(2,1)S(1)}, u32[]{:S(2)}, u32[]{:S(2)}) %collective-permute-start.2) | collective-permute-done | bytes 12320 | tf_op jit(solution)/shard_map/ppermute | solution.py:392
  63.2 0.0 collective-permute-done.1.near_2
  63.2 0.0 collective-permute-done.near_1
  63.2 0.0 copy-done.6
  63.2 0.8 shard_map.177
  64.1 0.4 all-to-all-done.3.gathered
  64.5 1.1 %shard_map.180 = bf16[16,32,384]{2,1,0:T(8,128)(2,1)S(1)} custom-call(bf16[16,72,128]{2,1,0:T(8,128)(2,1)S(1)} %all-to-all-done.3.gathered, f32[64,128]{1,0:T(8,128)S(1)} %get-tuple-element.37.own_weighted, f32[8,128]{1,0:T(8,128)S(1)} %get-tuple-element.38.own_stats, bf16[256,5120]{1,0:T(8,128)(2,1)S(1)} %shard_map.178.output_w, ...), custom_call_target="tpu_custom_call" | custom-call | tf_op jit(solution)/shard_map/pallas_call | solution.py:34
  65.6 17.8 %all_to_all.27.gathered = bf16[16,32,384]{2,1,0:T(8,128)(2,1)S(1)} all-to-all(bf16[16,32,384]{2,1,0:T(8,128)(2,1)S(1)} %shard_map.180), channel_id=1, replica_groups=mesh['group'=16,'tp'=16] {'tp'}, dimensions={0} | all-to-all | bytes 786432 | tf_op jit(solution)/shard_map/all_to_all | solution.py:306
  83.4 0.8 shard_map.181
  (7 shorter events, 0.0 us)
Async XLA Ops:
  0.0 33.6 %copy-start.5 = (bf16[128]{0:T(256)(128)(2,1)S(1)}, bf16[128]{0:T(256)(128)(2,1)}, u32[]{:S(2)}) copy-start(bf16[128]{0:T(256)(128)(2,1)} %gain.2) | copy-start | bytes 772
  1.6 14.7 %all-to-all-start = ((bf16[16,24,384]{2,1,0:T(8,128)(2,1)}), bf16[16,24,384]{2,1,0:T(8,128)(2,1)S(1)}, u32[]{:S(2)}, u32[]{:S(2)}) async-start(bf16[16,24,384]{2,1,0:T(8,128)(2,1)} %shard_map.172), calls=%async_computation | async-start | bytes 589824 | tf_op jit(solution)/shard_map/all_to_all | solution.py:306
  9.1 0.7 copy-start.2
  9.8 0.7 copy-start.3
  10.5 0.7 copy-start.7
  11.1 35.6 %copy-start = (bf16[8,128,512]{2,1,0:T(8,128)(2,1)S(1)}, bf16[8,128,512]{2,1,0:T(8,128)(2,1)}, u32[]{:S(2)}) copy-start(bf16[8,128,512]{2,1,0:T(8,128)(2,1)} %keys.1) | copy-start | bytes 3145732
  11.1 35.6 %copy-start.1 = (bf16[8,128,512]{2,1,0:T(8,128)(2,1)S(1)}, bf16[8,128,512]{2,1,0:T(8,128)(2,1)}, u32[]{:S(2)}) copy-start(bf16[8,128,512]{2,1,0:T(8,128)(2,1)} %values.1) | copy-start | bytes 3145732
  11.1 35.6 %copy-start.4 = (s32[8]{0:T(128)S(1)}, s32[8]{0:T(128)}, u32[]{:S(2)}) copy-start(s32[8]{0:T(128)} %lengths.3) | copy-start | bytes 100
  49.1 15.3 %all-to-all-start.3 = ((bf16[16,72,128]{2,1,0:T(8,128)(2,1)}), bf16[16,72,128]{2,1,0:T(8,128)(2,1)S(1)}, u32[]{:S(2)}, u32[]{:S(2)}) async-start(bf16[16,72,128]{2,1,0:T(8,128)(2,1)} %shard_map.176), calls=%async_computation.3 | async-start | bytes 589824 | tf_op jit(solution)/shard_map/all_to_all | solution.py:306
  53.7 9.5 %collective-permute-start.2 = (bf16[48,128]{1,0:T(8,128)(2,1)S(1)}, bf16[48,128]{1,0:T(8,128)(2,1)S(1)}, u32[]{:S(2)}, u32[]{:S(2)}) collective-permute-start(bf16[48,128]{1,0:T(8,128)(2,1)S(1)} %get-tuple-element.35.near), channel_id=1, source_target_pairs={{0,3},{1,2},{2,1},{3,0},{4,7},{5,6},{6,5},{7,4},{8,11},{9,10},{10,... | collective-permute-start | bytes 36872 | tf_op jit(solution)/shard_map/ppermute | solution.py:392
  57.4 5.8 %collective-permute-start.1 = (bf16[48,128]{1,0:T(8,128)(2,1)S(1)}, bf16[48,128]{1,0:T(8,128)(2,1)S(1)}, u32[]{:S(2)}, u32[]{:S(2)}) collective-permute-start(bf16[48,128]{1,0:T(8,128)(2,1)S(1)} %get-tuple-element.35.near), channel_id=1, source_target_pairs={{0,2},{1,3},{2,0},{3,1},{4,6},{5,7},{6,4},{7,5},{8,10},{9,11},{10,... | collective-permute-start | bytes 36872 | tf_op jit(solution)/shard_map/ppermute | solution.py:392
  57.4 5.8 %collective-permute-start = (bf16[48,128]{1,0:T(8,128)(2,1)S(1)}, bf16[48,128]{1,0:T(8,128)(2,1)S(1)}, u32[]{:S(2)}, u32[]{:S(2)}) collective-permute-start(bf16[48,128]{1,0:T(8,128)(2,1)S(1)} %get-tuple-element.35.near), channel_id=1, source_target_pairs={{0,1},{1,0},{2,3},{3,2},{4,5},{5,4},{6,7},{7,6},{8,9},{9,8},{10,11... | collective-permute-start | bytes 36872 | tf_op jit(solution)/shard_map/ppermute | solution.py:392
  58.2 5.0 %copy-start.6 = (bf16[128]{0:T(256)(128)(2,1)S(1)}, bf16[128]{0:T(256)(128)(2,1)}, u32[]{:S(2)}) copy-start(bf16[128]{0:T(256)(128)(2,1)} %gain.3) | copy-start | bytes 772
